TPU v7x, 32 devices: a whole 2x2x4 slice. The times are simulated.
32 devices in a mesh: replica: 2 (over y), fsdp: 16 (over z, x, core).
Axes of the slice: x: 2, y: 2, z: 4, core: 2. Of those that a mesh axis runs over, the one named last changes fastest.
Arguments:
- tokens: bfloat16 [2, 2048, 6144], P('replica', 'fsdp'), may hold values from -6 to 6
- grad_out: bfloat16 [2, 2048, 6144], P('replica', 'fsdp'), may hold values from -6 to 6
- expert_ids: int32 [2, 2048, 2], P('replica', 'fsdp'), may hold values from 0 to 7, as said below
- gate_share: float32 [2, 2048], P('replica', 'fsdp'), may hold values from 0.05 to 0.95
- up_weight: bfloat16 [2, 6144, 8192], P('replica', None, 'fsdp'), may hold values from -0.078125 to 0.078125
- down_weight: bfloat16 [2, 8192, 6144], P('replica', 'fsdp'), may hold values from -0.0625 to 0.0625
- local_keys: float32 [2, 6144, 512], P('replica', 'fsdp'), may hold values from -6 to 6
- outer_keys: float32 [6144, 512], P('fsdp'), may hold values from -6 to 6
- momentum: float32 [6144, 512], P('fsdp', 'replica'), may hold values from -4 to 4
Outputs:
- input_grad: bfloat16 [2, 2048, 6144], P('replica', 'fsdp')
- new_outer: float32 [6144, 512], P('fsdp')
- new_momentum: float32 [6144, 512], P('fsdp', 'replica')
- outer_copy: bfloat16 [6144, 512], P('fsdp')
Inputs may be any that keep to these rules, and one draw needn't show every extreme that they name: `expert_ids`: every token names two different experts. In each replica, each device's 128 consecutive tokens hold exactly 16 that name expert 0.
All inputs are finite; a program needn't handle non-finite values.
Results may differ from a plain program's by a relative error of at most 0.0049.
Values may be sent and summed in bfloat16 or wider, within the bound.
A program may use at most 128 MiB of HBM per device.

v0:
```python
import jax
import jax.numpy as jnp
from jax import lax
from jax.sharding import PartitionSpec as P

CAP = 16


outer_beta = 0.9
outer_rate = 0.7


def transposed(left, right):
    return lax.dot_general(
        left, right, (((1,), (1,)), ((), ())), preferred_element_type=jnp.float32
    )


def silu_grad(back, pre):
    sig = jax.nn.sigmoid(pre)
    return (back * sig * (1.0 + pre * (1.0 - sig))).astype(jnp.bfloat16)


def per_device(
    tokens,
    grad_out,
    expert_ids,
    gate_share,
    up_weight,
    down_weight,
    local_keys,
    outer_keys,
    momentum,
):
    outer_term = outer_keys - local_keys[0]
    total = lax.psum(outer_term, "replica")
    width = momentum.shape[1]
    share = lax.dynamic_slice_in_dim(total, lax.axis_index("replica") * width, width, 1)
    pseudo = share / lax.axis_size("replica")
    new_momentum = outer_beta * momentum + pseudo
    step_share = pseudo + outer_beta * new_momentum
    full_step = lax.all_gather(step_share, "replica", axis=1, tiled=True)
    new_outer = outer_keys - outer_rate * full_step
    inputs = tokens[0]
    grads = grad_out[0]
    ids_local = expert_ids[0]
    share_local = gate_share[0]
    up_local = up_weight[0]
    down_local = down_weight[0]
    first = ids_local[:, 0] == 0
    second = ids_local[:, 1] == 0
    coef = jnp.where(first, share_local, jnp.where(second, 1.0 - share_local, 0.0))
    picked = jnp.nonzero(first | second, size=CAP)[0].astype(jnp.int32)
    rows_in = inputs[picked]
    rows_grad = grads[picked]
    every_in, every_grad = (
        lax.all_gather(rows_in, "fsdp", axis=0, tiled=True),
        lax.all_gather(rows_grad, "fsdp", axis=0, tiled=True),
    )
    pre = jnp.dot(every_in, up_local, preferred_element_type=jnp.float32)
    hidden_grad = silu_grad(transposed(every_grad, down_local), pre)
    piece = lax.slice_in_dim(hidden_grad, 0, CAP * lax.axis_size("fsdp"), axis=0)
    summed = lax.psum_scatter(transposed(piece, up_local), "fsdp", scatter_dimension=0, tiled=True)
    result = (coef[picked][:, None] * summed).astype(jnp.bfloat16)
    input_grad = jnp.zeros(inputs.shape, jnp.bfloat16).at[picked].set(result)
    return (input_grad[None], new_outer, new_momentum, new_outer.astype(jnp.bfloat16))


def solution(mesh):
    placed = (
        P("replica", "fsdp", None),
        P("replica", "fsdp", None),
        P("replica", "fsdp", None),
        P("replica", "fsdp"),
        P("replica", None, "fsdp"),
        P("replica", "fsdp", None),
        P("replica", "fsdp", None),
        P("fsdp", None),
        P("fsdp", "replica"),
    )
    return jax.shard_map(
        per_device,
        mesh=mesh,
        in_specs=placed,
        out_specs=(
            P("replica", "fsdp", None),
            P("fsdp", None),
            P("fsdp", "replica"),
            P("fsdp", None),
        ),
        check_vma=False,
    )
```

profile of v0, /device:TPU:0, one launch (start us, length us, event | category | flops | bytes accessed | tf_op | source)
XLA Modules:
  0.0 216.0 jit_solution(18357454449834833546)
XLA Ops:
  8.0 0.0 copy-start
  8.0 0.0 copy-start.2
  8.0 0.0 copy-start.1
  8.0 0.0 all-gather.7.cloned.1.call-start
  8.1 0.9 copy.15
  9.0 0.2 fusion.27
  9.2 0.2 reduce-window.6
  9.4 0.1 fusion.18
  9.5 1.4 scatter_custom_fusion
  10.9 0.1 copy.16
  11.1 0.6 fusion.22
  11.7 0.8 fusion.21
  12.5 0.0 copy-done
  12.5 1.3 gather_fusion.2
  13.8 0.0 all-gather.7.cloned.1.call-update
  13.8 0.0 all-gather.5.cloned.1.call-start
  13.9 3.1 %gather_fusion.1 = bf16[16,6144]{1,0:T(8,128)(2,1)} fusion(bf16[128,6144]{1,0:T(8,128)(2,1)} %bitcast.33, s32[1024]{0:T(1024)S(1)} %pad_clamp_fusion), kind=kCustom, calls=%fused_computation.1 | custom fusion | bytes 393280 | tf_op jit(solution)/shard_map/gather | solution.py:55
  17.0 0.0 all-gather.5.cloned.1.call-update
  17.1 0.0 all-reduce.2.cloned.1.call-start
  17.1 0.0 copy-done.2
  17.1 0.0 copy-done.1
  17.1 1.0 bitcast_subtract_fusion
  18.1 0.0 all-reduce.2.cloned.1.call-update
  18.2 0.0 reduce-scatter.2.cloned.1.call-start
  18.2 43.9 %all-gather.7.cloned.1.call-done = bf16[256,6144]{1,0:T(8,128)(2,1)} async-done(((bf16[16,6144]{1,0:T(8,128)(2,1)}), bf16[256,6144]{1,0:T(8,128)(2,1)}) %all-gather.7.cloned.1.call-update) | async-done | bytes 3145744 | tf_op jit(solution)/shard_map/all_gather | solution.py:57
  62.1 5.5 %fusion.2 = f32[256,512]{1,0:T(8,128)S(1)} fusion(bf16[256,6144]{1,0:T(8,128)(2,1)} %all-gather.7.cloned.1.call-done, bf16[1,6144,512]{2,1,0:T(8,128)(2,1)} %param.13), kind=kOutput, calls=%fused_computation.7 | convolution fusion | flops 1610612736 | bytes 9961472 | tf_op jit(solution)/shard_map/dot_general | solution.py:60
  67.6 41.4 %all-gather.5.cloned.1.call-done = bf16[256,6144]{1,0:T(8,128)(2,1)} async-done(((bf16[16,6144]{1,0:T(8,128)(2,1)}), bf16[256,6144]{1,0:T(8,128)(2,1)}) %all-gather.5.cloned.1.call-update) | async-done | bytes 3145744 | tf_op jit(solution)/shard_map/all_gather | solution.py:58
  109.0 5.6 %fusion.12 = bf16[256,512]{1,0:T(8,128)(2,1)S(1)} fusion(bf16[256,6144]{1,0:T(8,128)(2,1)} %all-gather.5.cloned.1.call-done, bf16[1,512,6144]{2,1,0:T(8,128)(2,1)} %param.14, f32[256,512]{1,0:T(8,128)S(1)} %fusion.2), kind=kOutput, calls=%fused_computation.13 | convolution fusion | flops 1611792384 | bytes 10223616 | tf_op jit(solution)/shard_map/dot_general | solution.py:14
  114.6 7.3 %fusion = f32[256,6144]{1,0:T(8,128)} fusion(bf16[256,512]{1,0:T(8,128)(2,1)S(1)} %fusion.12, bf16[1,6144,512]{2,1,0:T(8,128)(2,1)} %param.13), kind=kOutput, calls=%fused_computation.5 | convolution fusion | flops 1610612736 | bytes 12845056 | tf_op jit(solution)/shard_map/dot_general | solution.py:14
  121.9 0.0 copy-start.4
  121.9 0.0 copy-start.3
  121.9 0.0 reduce-scatter.2.cloned.1.call-update
  121.9 0.6 copy-done.4
  122.6 0.7 gather_fusion
  123.2 0.0 all-reduce.2.cloned.1.call-done
  123.3 0.0 copy-done.3
  123.3 1.8 multiply_add_fusion
  125.1 11.9 %all_gather.11 = f32[384,512]{1,0:T(8,128)S(1)} all-gather(f32[384,256]{1,0:T(8,128)S(1)} %get-tuple-element.6), channel_id=1, replica_groups=mesh['replica'=2,'fsdp'=16] {'replica'}, dimensions={1}, use_global_device_ids=true | all-gather | bytes 1179648 | tf_op jit(solution)/shard_map/all_gather | solution.py:42
  137.0 1.2 fusion.26
  138.2 67.9 %reduce-scatter.2.cloned.1.call-done = f32[16,6144]{1,0:T(8,128)} async-done(((f32[256,6144]{1,0:T(8,128)}), f32[16,6144]{1,0:T(8,128)}) %reduce-scatter.2.cloned.1.call-update) | async-done | bytes 393232 | tf_op jit(solution)/shard_map/reduce_scatter | solution.py:63
  206.1 2.8 %scatter_custom_fusion.1 = bf16[128,6144]{1,0:T(8,128)(2,1)} fusion(s32[16]{0:T(128)S(1)} %fusion.21, bf16[]{:T(256)} %constant.27.clone.1, f32[16,6144]{1,0:T(8,128)} %reduce-scatter.2.cloned.1.call-done, f32[16]{0:T(128)S(1)} %gather_fusion), kind=kCustom, calls=%fused_computation.16 | custom fusion | flops 196608 | bytes 1966594 | tf_op jit(solution)/shard_map/scatter | solution.py:65
  (5 shorter events, 0.1 us)
Async XLA Ops:
  8.0 4.5 %copy-start = (bf16[1,128,6144]{2,1,0:T(8,128)(2,1)S(1)}, bf16[1,128,6144]{2,1,0:T(8,128)(2,1)}, u32[]{:S(2)}) copy-start(bf16[1,128,6144]{2,1,0:T(8,128)(2,1)} %param.9) | copy-start | bytes 4718596
  8.0 9.1 %copy-start.2 = (f32[1,384,512]{2,1,0:T(8,128)S(1)}, f32[1,384,512]{2,1,0:T(8,128)}, u32[]{:S(2)}) copy-start(f32[1,384,512]{2,1,0:T(8,128)} %param.15) | copy-start | bytes 2359300
  8.0 9.1 %copy-start.1 = (f32[384,512]{1,0:T(8,128)S(1)}, f32[384,512]{1,0:T(8,128)}, u32[]{:S(2)}) copy-start(f32[384,512]{1,0:T(8,128)} %param.16) | copy-start | bytes 2359300
  8.0 54.1 %all-gather.7.cloned.1.call-start = ((), (), s32[]{:S(2)}) async-start(), calls=%async_computation.4 | async-start | bytes 3342336 | tf_op jit(solution)/shard_map/all_gather | solution.py:57
  13.8 95.2 %all-gather.5.cloned.1.call-start = ((), (), s32[]{:S(2)}) async-start(), calls=%async_computation.3 | async-start | bytes 3342336 | tf_op jit(solution)/shard_map/all_gather | solution.py:58
  17.1 106.2 %all-reduce.2.cloned.1.call-start = ((), (), s32[]{:S(2)}) async-start(), calls=%async_computation.2 | async-start | bytes 1572864 | tf_op jit(solution)/shard_map/psum | solution.py:36
  18.2 187.9 %reduce-scatter.2.cloned.1.call-start = ((), (), s32[]{:S(2)}) async-start(), calls=%async_computation.1 | async-start | bytes 6684672 | tf_op jit(solution)/shard_map/reduce_scatter | solution.py:63
  121.9 0.7 copy-start.4
  121.9 1.4 copy-start.3
Sparse Core Ops, SparseCore 0:
  14.0 48.0 all-gather.6
  65.0 43.9 all-gather.4
  122.1 83.9 reduce-scatter.1
Sparse Core Ops, SparseCore 1:
  20.5 36.8 all-reduce.1
where the time goes:
time: 216 us
  waiting for transfers between devices  153 us (71%)
  matrix products  18.4 us (9%)
  between operations  15.3 us (7%)
  blocking collectives  11.9 us (6%)
  other arithmetic  10.2 us (5%)
  local copies, waits for them, and re-layouts  6.81 us (3%)
    reduce_scatter x1, waiting for transfers between devices, per_device(): lax.psum_scatter(transposed(piece, up_local), 'fsdp', scatter_dimension=0...  67.9 us
    all_gather x1, waiting for transfers between devices, per_device(): lax.all_gather(rows_in, 'fsdp', axis=0, tiled=True)  43.9 us
    all_gather x1, waiting for transfers between devices, per_device(): lax.all_gather(rows_grad, 'fsdp', axis=0, tiled=True)  41.4 us
    dot_general x2, matrix products, transposed(): lax.dot_general(left, right, (((1,), (1,)), ((), ())), preferred_element_...  12.9 us
    all_gather x1, blocking collectives, per_device(): full_step = lax.all_gather(step_share, 'replica', axis=1, tiled=True)  11.9 us
    dot_general x1, matrix products, per_device(): pre = jnp.dot(every_in, up_local, preferred_element_type=jnp.float32)  5.52 us
  transfers between devices with their start and end apart: 4, of which 3 were waited for; matrix products, arithmetic and copies ran while one was open for 12% of the time, Pallas kernels for 0%

commit v1 on v0

v1 whole, which is shorter than its diff:
```python
import functools

import jax
import jax.numpy as jnp
from jax import lax
from jax.experimental import pallas as pl
from jax.experimental.pallas import tpu as pltpu
from jax.sharding import PartitionSpec as P

CAP = 16
MAJOR = 4
PIECES = 8
KEY_PIECES = 8

outer_beta = 0.9
outer_rate = 0.7

MESH = pl.DeviceIdType.MESH


def dot_nn(left, right):
    return jnp.dot(left, right, preferred_element_type=jnp.float32)


def dot_nt(left, right):
    return lax.dot_general(
        left, right, (((1,), (1,)), ((), ())), preferred_element_type=jnp.float32
    )


def staged(count, stages):
    def step(t, carry):
        for lag, stage in stages:
            piece = t - lag

            @pl.when((piece >= 0) & (piece < count))
            def _():
                stage(piece)

        return carry

    lax.fori_loop(0, count + max(lag for lag, _ in stages), step, 0)


def kernel(
    R,
    A,
    B,
    K,
    ids_ref,
    share_ref,
    tok_ref,
    grad_ref,
    up_ref,
    down_ref,
    local_ref,
    mom_ref,
    res_ref,
    sel_out_ref,
    local_all,
    mom_all,
    src,
    buf,
    upv,
    downv,
    sel_ref,
    coef_ref,
    pre_ref,
    back_ref,
    hid_ref,
    part,
    sib_out,
    sib_in,
    x_out,
    x_in,
    z_out,
    z_in,
    src_sem,
    up_sem,
    down_sem,
    own_sem,
    y_send,
    y_recv,
    gz_send,
    gz_recv,
    gx_send,
    gx_recv,
    gs_send,
    gs_recv,
    rs_send,
    rs_recv,
    rx_send,
    rx_recv,
    rz_send,
    rz_recv,
):
    r = lax.axis_index("replica")
    me = lax.axis_index("fsdp")
    c = lax.rem(me, 2)
    b = lax.rem(me // 2, B)
    a = me // (2 * B)
    NP = 2 * K
    width = src.shape[-1]
    column = A * CAP
    half = B * column

    def at(a_, b_, c_):
        return (r, (a_ * B + b_) * 2 + c_)

    sibling = at(a, b, 1 - c)
    z_peers = [at(lax.rem(a + j, A), b, c) for j in range(1, A)]
    x_peers = [at(a, lax.rem(b + j, B), c) for j in range(1, B)]
    y_peers = [(lax.rem(r + j, R), me) for j in range(1, R)]

    for k in range(K):
        cols = pl.ds(k * width, width)
        pltpu.make_async_copy(tok_ref.at[:, cols], src.at[k], src_sem.at[k]).start()
    for k in range(K):
        cols = pl.ds(k * width, width)
        pltpu.make_async_copy(up_ref.at[cols], upv.at[k], up_sem.at[k]).start()
    for k in range(K):
        cols = pl.ds(k * width, width)
        pltpu.make_async_copy(grad_ref.at[:, cols], src.at[K + k], src_sem.at[K + k]).start()
    for k in range(K):
        cols = pl.ds(k * width, width)
        pltpu.make_async_copy(down_ref.at[:, cols], downv.at[k], down_sem.at[k]).start()
    own_local = pltpu.make_async_copy(local_ref, local_all.at[r], own_sem.at[0])
    own_mom = pltpu.make_async_copy(mom_ref, mom_all.at[r], own_sem.at[1])
    own_local.start()
    own_mom.start()

    barrier = pltpu.get_barrier_semaphore()
    peers = [sibling] + z_peers + x_peers + y_peers
    for peer in peers:
        pl.semaphore_signal(barrier, inc=1, device_id=peer, device_id_type=MESH)

    T = ids_ref.shape[0]
    ids = ids_ref[...]
    first = (ids[:, 0:1] == 0).astype(jnp.float32)
    second = (ids[:, 1:2] == 0).astype(jnp.float32)
    named = jnp.broadcast_to(first + second, (T, T))
    row = lax.broadcasted_iota(jnp.int32, (T, T), 0)
    col = lax.broadcasted_iota(jnp.int32, (T, T), 1)
    below = jnp.where(col < row, 1.0, 0.0).astype(jnp.bfloat16)
    rank = dot_nn(below, named.astype(jnp.bfloat16))
    sel_t = jnp.where((rank == col.astype(jnp.float32)) & (named > 0.5), 1.0, 0.0)
    sel_out_ref[...] = sel_t.astype(jnp.bfloat16)
    sel = sel_t.T
    sel_ref[...] = sel[:CAP].astype(jnp.bfloat16)
    first_row = jnp.broadcast_to(first, (T, T)).T
    share = share_ref[...]
    coef = jnp.where(first_row[:CAP] > 0.5, share, 1.0 - share)
    coef_ref[...] = jnp.broadcast_to(
        jnp.sum(sel[:CAP] * coef, axis=1, keepdims=True), coef_ref.shape
    )
    pre_ref[...] = jnp.zeros_like(pre_ref)
    back_ref[...] = jnp.zeros_like(back_ref)

    pl.semaphore_wait(barrier, len(peers))

    def remote(source, target, send, recv, peer):
        return pltpu.make_async_remote_copy(
            src_ref=source,
            dst_ref=target,
            send_sem=send,
            recv_sem=recv,
            device_id=peer,
            device_id_type=MESH,
        )

    def rows_of(b_):
        return pl.ds(pl.multiple_of((c * B + b_) * column, column), column)

    def gz(p):
        mine = buf.at[p, pl.ds(pl.multiple_of((c * B + b) * column + a * CAP, CAP), CAP)]
        return [
            remote(mine, mine, gz_send.at[p, j], gz_recv.at[p, j], z_peers[j])
            for j in range(A - 1)
        ]

    def gx(p):
        mine = buf.at[p, rows_of(b)]
        return [
            remote(mine, mine, gx_send.at[p, j], gx_recv.at[p, j], x_peers[j])
            for j in range(B - 1)
        ]

    def gs(p, j):
        part_of = buf.at[p, rows_of(lax.rem(b + j, B))]
        return remote(part_of, part_of, gs_send.at[p, j], gs_recv.at[p, j], sibling)

    key_rows = local_ref.shape[0] // KEY_PIECES

    def ys(p):
        rows = pl.ds(pl.multiple_of(p * key_rows, 8), key_rows)
        copies = []
        for j in range(R - 1):
            copies.append(
                remote(local_ref.at[rows], local_all.at[r, rows], y_send.at[p, j, 0], y_recv.at[p, j, 0], y_peers[j])
            )
            copies.append(
                remote(mom_ref.at[rows], mom_all.at[r, rows], y_send.at[p, j, 1], y_recv.at[p, j, 1], y_peers[j])
            )
        return copies

    def pick(p):
        pltpu.make_async_copy(tok_ref.at[:, pl.ds(0, width)], src.at[p], src_sem.at[p]).wait()
        rows = pl.ds(pl.multiple_of((c * B + b) * column + a * CAP, CAP), CAP)
        buf[p, rows, :] = dot_nn(sel_ref[...], src[p]).astype(jnp.bfloat16)
        for copy in gz(p):
            copy.start()

        @pl.when(p < KEY_PIECES)
        def _():
            for copy in ys(p):
                copy.start()

    def across(p):
        for copy in gz(p):
            copy.wait_recv()
        for copy in gx(p):
            copy.start()
        gs(p, 0).start()

    def aside(p):
        for j, copy in enumerate(gx(p)):
            copy.wait_recv()
            gs(p, B - 1 - j).start()

    def multiply(p):
        for j in range(B):
            gs(p, j).wait_recv()

        @pl.when(p < K)
        def _():
            pltpu.make_async_copy(up_ref.at[pl.ds(0, width)], upv.at[p], up_sem.at[p]).wait()
            pre_ref[...] += dot_nn(buf[p], upv[p])

        @pl.when(p >= K)
        def _():
            k = p - K
            pltpu.make_async_copy(
                down_ref.at[:, pl.ds(0, width)], downv.at[k], down_sem.at[k]
            ).wait()
            back_ref[...] += dot_nt(buf[p], downv[k])

    staged(NP, [(0, pick), (2, across), (4, aside), (5, multiply)])

    pre = pre_ref[...]
    sig = jax.nn.sigmoid(pre)
    hid_ref[...] = (back_ref[...] * sig * (1.0 + pre * (1.0 - sig))).astype(jnp.bfloat16)

    own_half = pl.ds(pl.multiple_of(c * half, half), half)
    other_half = pl.ds(pl.multiple_of((1 - c) * half, half), half)

    def rs(q):
        return remote(sib_out.at[q], sib_in.at[q], rs_send.at[q], rs_recv.at[q], sibling)

    def rx(q):
        return [
            remote(x_out.at[q, j], x_in.at[q, j], rx_send.at[q, j], rx_recv.at[q, j], x_peers[j])
            for j in range(B - 1)
        ]

    def rz(q):
        return [
            remote(z_out.at[q, j], z_in.at[q, j], rz_send.at[q, j], rz_recv.at[q, j], z_peers[j])
            for j in range(A - 1)
        ]

    def produce(q):
        part[q] = dot_nt(hid_ref[...], upv[q])
        sib_out[q] = part[q, other_half, :].astype(jnp.bfloat16)
        rs(q).start()

    def pair(q):
        rs(q).wait_recv()
        for j, copy in enumerate(rx(q)):
            b_ = lax.rem(b + j + 1, B)
            there = pl.ds(pl.multiple_of(b_ * column, column), column)
            mine = part[q, pl.ds(pl.multiple_of(c * half + b_ * column, column), column), :]
            x_out[q, j] = (mine + sib_in[q, there, :].astype(jnp.float32)).astype(jnp.bfloat16)
            copy.start()

    def chain(q):
        here = pl.ds(pl.multiple_of(b * column, column), column)
        mine = pl.ds(pl.multiple_of(c * half + b * column, column), column)
        total = part[q, mine, :] + sib_in[q, here, :].astype(jnp.float32)
        for j, copy in enumerate(rx(q)):
            copy.wait_recv()
            total = total + x_in[q, j].astype(jnp.float32)
        part[q, mine, :] = total
        for j, copy in enumerate(rz(q)):
            a_ = lax.rem(a + j + 1, A)
            rows = pl.ds(pl.multiple_of(c * half + b * column + a_ * CAP, CAP), CAP)
            z_out[q, j] = part[q, rows, :].astype(jnp.bfloat16)
            copy.start()

    def finish(q):
        rows = pl.ds(pl.multiple_of(c * half + b * column + a * CAP, CAP), CAP)
        total = part[q, rows, :]
        for j, copy in enumerate(rz(q)):
            copy.wait_recv()
            total = total + z_in[q, j].astype(jnp.float32)
        cols = pl.ds(pl.multiple_of(q * width, 128), width)
        res_ref[:, cols] = (coef_ref[:, 0:1] * total).astype(jnp.bfloat16)

    staged(K, [(0, produce), (1, pair), (3, chain), (5, finish)])

    def sent_gather(p, carry):
        for copy in gz(p) + gx(p) + [gs(p, j) for j in range(B)]:
            copy.wait_send()
        return carry

    def sent_reduce(q, carry):
        for copy in [rs(q)] + rx(q) + rz(q):
            copy.wait_send()
        return carry

    def keys_done(p, carry):
        for copy in ys(p):
            copy.wait()
        return carry

    lax.fori_loop(0, NP, sent_gather, 0)
    lax.fori_loop(0, K, sent_reduce, 0)
    lax.fori_loop(0, KEY_PIECES, keys_done, 0)
    own_local.wait()
    own_mom.wait()


def exchange(R, F, ids, share, tokens, grads, up, down, local, momentum):
    A = MAJOR
    B = F // (2 * A)
    K = PIECES
    D = tokens.shape[1]
    H = up.shape[1]
    T = tokens.shape[0]
    width = D // K
    rows = F * CAP
    column = A * CAP
    half = B * column
    dma = pltpu.SemaphoreType.DMA
    vmem = pl.BlockSpec(memory_space=pltpu.VMEM)
    hbm = pl.BlockSpec(memory_space=pl.ANY)
    return pl.pallas_call(
        functools.partial(kernel, R, A, B, K),
        out_shape=(
            jax.ShapeDtypeStruct((CAP, D), jnp.bfloat16),
            jax.ShapeDtypeStruct((T, T), jnp.bfloat16),
            jax.ShapeDtypeStruct((R,) + local.shape, jnp.float32),
            jax.ShapeDtypeStruct((R,) + momentum.shape, jnp.float32),
        ),
        in_specs=[vmem, vmem, hbm, hbm, hbm, hbm, hbm, hbm],
        out_specs=(vmem, vmem, hbm, hbm),
        scratch_shapes=[
            pltpu.VMEM((2 * K, T, width), jnp.bfloat16),
            pltpu.VMEM((2 * K, rows, width), jnp.bfloat16),
            pltpu.VMEM((K, width, H), jnp.bfloat16),
            pltpu.VMEM((K, H, width), jnp.bfloat16),
            pltpu.VMEM((CAP, T), jnp.bfloat16),
            pltpu.VMEM((CAP, 128), jnp.float32),
            pltpu.VMEM((rows, H), jnp.float32),
            pltpu.VMEM((rows, H), jnp.float32),
            pltpu.VMEM((rows, H), jnp.bfloat16),
            pltpu.VMEM((K, rows, width), jnp.float32),
            pltpu.VMEM((K, half, width), jnp.bfloat16),
            pltpu.VMEM((K, half, width), jnp.bfloat16),
            pltpu.VMEM((K, B - 1, column, width), jnp.bfloat16),
            pltpu.VMEM((K, B - 1, column, width), jnp.bfloat16),
            pltpu.VMEM((K, A - 1, CAP, width), jnp.bfloat16),
            pltpu.VMEM((K, A - 1, CAP, width), jnp.bfloat16),
            dma((2 * K,)),
            dma((K,)),
            dma((K,)),
            dma((2,)),
            dma((KEY_PIECES, R - 1, 2)),
            dma((KEY_PIECES, R - 1, 2)),
            dma((2 * K, A - 1)),
            dma((2 * K, A - 1)),
            dma((2 * K, B - 1)),
            dma((2 * K, B - 1)),
            dma((2 * K, B)),
            dma((2 * K, B)),
            dma((K,)),
            dma((K,)),
            dma((K, B - 1)),
            dma((K, B - 1)),
            dma((K, A - 1)),
            dma((K, A - 1)),
        ],
        compiler_params=pltpu.CompilerParams(
            collective_id=0, has_side_effects=True, vmem_limit_bytes=60 * 1024 * 1024
        ),
        cost_estimate=pl.CostEstimate(
            flops=6 * rows * D * H, bytes_accessed=8 * D * H, transcendentals=rows * H
        ),
    )(ids, share, tokens, grads, up, down, local, momentum)


def per_device(
    R,
    F,
    tokens,
    grad_out,
    expert_ids,
    gate_share,
    up_weight,
    down_weight,
    local_keys,
    outer_keys,
    momentum,
):
    result, sel, local_all, mom_all = exchange(
        R,
        F,
        expert_ids[0],
        gate_share,
        tokens[0],
        grad_out[0],
        up_weight[0],
        down_weight[0],
        local_keys[0],
        momentum,
    )
    input_grad = jnp.dot(
        sel[:, :CAP], result, preferred_element_type=jnp.float32
    ).astype(jnp.bfloat16)
    pseudo = outer_keys - local_all[0]
    for one in range(1, R):
        pseudo = pseudo + (outer_keys - local_all[one])
    pseudo = pseudo / R
    every = jnp.concatenate([mom_all[one] for one in range(R)], axis=1)
    moved = outer_beta * every + pseudo
    new_outer = outer_keys - outer_rate * (pseudo + outer_beta * moved)
    width = momentum.shape[1]
    new_momentum = lax.dynamic_slice_in_dim(moved, lax.axis_index("replica") * width, width, 1)
    return (input_grad[None], new_outer, new_momentum, new_outer.astype(jnp.bfloat16))


def solution(mesh):
    placed = (
        P("replica", "fsdp", None),
        P("replica", "fsdp", None),
        P("replica", "fsdp", None),
        P("replica", "fsdp"),
        P("replica", None, "fsdp"),
        P("replica", "fsdp", None),
        P("replica", "fsdp", None),
        P("fsdp", None),
        P("fsdp", "replica"),
    )
    return jax.shard_map(
        functools.partial(per_device, mesh.shape["replica"], mesh.shape["fsdp"]),
        mesh=mesh,
        in_specs=placed,
        out_specs=(
            P("replica", "fsdp", None),
            P("fsdp", None),
            P("fsdp", "replica"),
            P("fsdp", None),
        ),
        check_vma=False,
    )
```

time: 216 us -> 84.7 us (0.39)
  waiting for transfers between devices: 153 us -> 0 us
  Pallas kernels: 0 us -> 77 us
  matrix products: 18.4 us -> 1.69 us
  between operations: 15.3 us -> 0.66 us
  blocking collectives: 11.9 us -> 0 us
  other arithmetic: 10.2 us -> 1.36 us
  local copies, waits for them, and re-layouts: 6.81 us -> 3.82 us
    all_gather x2 -> x0, waiting for transfers between devices: 85.3 us -> none  [the longest x1 43.9 us: per_device(): lax.all_gather(rows_in, 'fsdp', axis=0, tiled=True)]
    pallas_call x0 -> x1, Pallas kernels: none -> 77 us  [exchange(): pl.pallas_call(functools.partial(kernel, R, A, B, K), out_shape=(jax.Shap...]
    reduce_scatter x1 -> x0, waiting for transfers between devices: 67.9 us -> none  [per_device(): lax.psum_scatter(transposed(piece, up_local), 'fsdp', scatter_dimension=0...]
    dot_general x3 -> x1, matrix products: 18.4 us -> 1.69 us  [per_device(): jnp.dot(sel[:, :CAP], result, preferred_element_type=jnp.float32)]
    all_gather x1 -> x0, blocking collectives: 11.9 us -> none  [per_device(): full_step = lax.all_gather(step_share, 'replica', axis=1, tiled=True)]
    gather x3 -> x0, local copies, waits for them, and re-layouts: 5.14 us -> none  [the longest x1 3.13 us: per_device(): rows_grad = grads[picked]]
    scatter x1 -> x0, other arithmetic: 2.81 us -> none  [per_device(): input_grad = jnp.zeros(inputs.shape, jnp.bfloat16).at[picked].set(result)]
  transfers between devices with their start and end apart: 4 -> 0, of which waited for: 3 -> 0; matrix products, arithmetic and copies ran while one was open for 12% -> 0% of each run, Pallas kernels for 0% -> 0%
where the time goes in v1:
time: 84.7 us; the launch traced here: 84.5 us
  Pallas kernels  77 us (91%)
  local copies, waits for them, and re-layouts  3.82 us (5%)
  matrix products  1.69 us (2%)
  other arithmetic  1.36 us (2%)
    pallas_call x1, Pallas kernels, exchange(): pl.pallas_call(functools.partial(kernel, R, A, B, K), out_shape=(jax.Shap...  77 us
    unnamed x9, local copies, waits for them, and re-layouts  1.76 us

profile of v1, /device:TPU:0, one launch (start us, length us, event | category | flops | bytes accessed | tf_op | source)
XLA Modules:
  0.0 84.5 jit_solution(12616024343733779293)
XLA Ops:
  0.6 1.4 %copy.13 = s32[1,128,2]{2,1,0:T(8,128)} copy(s32[1,128,2]{1,2,0:T(2,128)} %param.11) | data formatting | bytes 2048 | tf_op args[2]
  2.0 0.0 copy-start.1
  2.0 77.0 %shard_map.120 = (bf16[16,6144]{1,0:T(8,128)(2,1)}, bf16[128,128]{1,0:T(8,128)(2,1)}, f32[2,384,512]{2,1,0:T(8,128)}, f32[2,384,256]{2,1,0:T(8,128)}) custom-call(s32[128,2]{1,0:T(8,128)} %bitcast.35, f32[1,128]{1,0:T(1,128)} %share_ref.1, bf16[128,6144]{1,0:T(8,128)(2,1)} %bitcast.38, bf16[128,6144]{1,0:T(8,128)(2,1)} %bitcast.39, ...), custom_call_target="tpu_custom_call" | custom-call | flops 4831838208 | bytes 25165824 | tf_op jit(solution)/shard_map/pallas_call | solution.py:346
  79.1 0.0 copy-start
  79.1 1.3 %slice_bitcast_fusion.1 = (f32[384,256]{1,0:T(8,128)S(1)}, f32[384,256]{1,0:T(8,128)S(1)}) fusion(f32[2,384,256]{2,1,0:T(8,128)} %get-tuple-element.11), kind=kLoop, calls=%fused_computation.10 | loop fusion | bytes 1572864 | tf_op jit(solution)/shard_map/squeeze | solution.py:433
  80.4 0.0 copy-done.1
  80.4 0.3 copy-done
  80.7 0.0 copy-start.2
  80.7 0.0 copy-start.3
  80.7 1.4 %fusion.5 = (bf16[384,512]{1,0:T(8,128)(2,1)}, f32[384,512]{1,0:T(8,128)}, f32[384,512]{1,0:T(8,128)S(1)}) fusion(f32[384,512]{1,0:T(8,128)S(1)} %copy-done.1, f32[2,384,512]{2,1,0:T(8,128)S(1)} %copy-done, f32[384,256]{1,0:T(8,128)S(1)} %get-tuple-element.16, f32[384,256]{1,0:T(8,128)S(1)} %get-tuple-element.15), kind=kLoop, calls=%fused_computation.13 | loop fusion | flops 2359296 | bytes 5111808 | tf_op jit(solution)/shard_map/convert_element_type | solution.py:438
  82.1 0.8 constant_dynamic-slice_fusion
  82.8 0.0 copy-done.2
  82.8 0.0 copy-done.3
  82.8 1.7 %fusion = bf16[1,128,6144]{2,1,0:T(8,128)(2,1)} fusion(bf16[16,6144]{1,0:T(8,128)(2,1)S(1)} %copy-done.2, bf16[128,128]{1,0:T(8,128)(2,1)S(1)} %copy-done.3), kind=kOutput, calls=%fused_computation.1 | convolution fusion | flops 25952256 | bytes 1802240 | tf_op jit(solution)/shard_map/dot_general | solution.py:426
Async XLA Ops:
  2.0 78.3 %copy-start.1 = (f32[384,512]{1,0:T(8,128)S(1)}, f32[384,512]{1,0:T(8,128)}, u32[]{:S(2)}) copy-start(f32[384,512]{1,0:T(8,128)} %param.16) | copy-start | bytes 2359300
  79.1 1.6 %copy-start = (f32[2,384,512]{2,1,0:T(8,128)S(1)}, f32[2,384,512]{2,1,0:T(8,128)}, u32[]{:S(2)}) copy-start(f32[2,384,512]{2,1,0:T(8,128)} %get-tuple-element.10) | copy-start | bytes 4718596
  80.7 2.1 %copy-start.2 = (bf16[16,6144]{1,0:T(8,128)(2,1)S(1)}, bf16[16,6144]{1,0:T(8,128)(2,1)}, u32[]{:S(2)}) copy-start(bf16[16,6144]{1,0:T(8,128)(2,1)} %get-tuple-element.9) | copy-start | bytes 589828
  80.7 2.1 %copy-start.3 = (bf16[128,128]{1,0:T(8,128)(2,1)S(1)}, bf16[128,128]{1,0:T(8,128)(2,1)}, u32[]{:S(2)}) copy-start(bf16[128,128]{1,0:T(8,128)(2,1)} %get-tuple-element.8) | copy-start | bytes 98308

commit v2 on v1

v2 whole, which is shorter than its diff:
```python
import functools

import jax
import jax.numpy as jnp
from jax import lax
from jax.experimental import pallas as pl
from jax.experimental.pallas import tpu as pltpu
from jax.sharding import PartitionSpec as P

CAP = 16
MAJOR = 4
PIECES = 8
BACK_PIECES = 12
KEY_PIECES = 8
TAIL_STEPS = 4

outer_beta = 0.9
outer_rate = 0.7

MESH = pl.DeviceIdType.MESH


def dot_nn(left, right):
    return jnp.dot(left, right, preferred_element_type=jnp.float32)


def dot_nt(left, right):
    return lax.dot_general(
        left, right, (((1,), (1,)), ((), ())), preferred_element_type=jnp.float32
    )


def staged(count, stages):
    def step(t, carry):
        for lag, stage in stages:
            piece = t - lag

            @pl.when((piece >= 0) & (piece < count))
            def _():
                stage(piece)

        return carry

    lax.fori_loop(0, count + max(lag for lag, _ in stages), step, 0)


def kernel(
    R,
    B,
    K,
    KR,
    ids_ref,
    share_ref,
    tok_ref,
    grad_ref,
    up_ref,
    down_ref,
    local_ref,
    mom_ref,
    res_ref,
    sel_out_ref,
    local_all,
    mom_all,
    src,
    buf,
    upv,
    downv,
    sel_ref,
    coef_ref,
    pre_ref,
    back_ref,
    hid_ref,
    part,
    sib_out,
    sib_in,
    x_out,
    x_in,
    n_out,
    n_in,
    m_out,
    m_in,
    d_out,
    d_in,
    src_sem,
    up_sem,
    down_sem,
    own_sem,
    y_send,
    y_recv,
    g_send,
    g_recv,
    r_send,
    r_recv,
):
    A = MAJOR
    r = lax.axis_index("replica")
    me = lax.axis_index("fsdp")
    c = lax.rem(me, 2)
    b = lax.rem(me // 2, B)
    a = me // (2 * B)
    NP = 2 * K
    width = src.shape[-1]
    column = A * CAP
    half = B * column
    a_mate = a + 1 - 2 * lax.rem(a, 2)
    a_diag = lax.rem(a + 2, A)
    a_cross = A - 1 - a
    a_pair = 2 - 2 * (a // 2)

    def at(a_, b_, c_):
        return (r, (a_ * B + b_) * 2 + c_)

    sibling = at(a, b, 1 - c)
    mate = at(a_mate, b, c)
    diag = at(a_diag, b, c)
    x_peers = [at(a, lax.rem(b + j, B), c) for j in range(1, B)]
    y_peers = [(lax.rem(r + j, R), me) for j in range(1, R)]

    for k in range(K):
        cols = pl.ds(k * width, width)
        pltpu.make_async_copy(tok_ref.at[:, cols], src.at[k], src_sem.at[k]).start()
    for k in range(K):
        cols = pl.ds(k * width, width)
        pltpu.make_async_copy(up_ref.at[cols], upv.at[cols], up_sem.at[k]).start()
    for k in range(K):
        cols = pl.ds(k * width, width)
        pltpu.make_async_copy(grad_ref.at[:, cols], src.at[K + k], src_sem.at[K + k]).start()
    for k in range(K):
        cols = pl.ds(k * width, width)
        pltpu.make_async_copy(down_ref.at[:, cols], downv.at[k], down_sem.at[k]).start()
    own_local = pltpu.make_async_copy(local_ref, local_all.at[r], own_sem.at[0])
    own_mom = pltpu.make_async_copy(mom_ref, mom_all.at[r], own_sem.at[1])
    own_local.start()
    own_mom.start()

    barrier = pltpu.get_barrier_semaphore()
    peers = [sibling, mate, diag] + x_peers + y_peers
    for peer in peers:
        pl.semaphore_signal(barrier, inc=1, device_id=peer, device_id_type=MESH)

    T = ids_ref.shape[1]
    first = (ids_ref[0:1, :] == 0).astype(jnp.float32)
    second = (ids_ref[1:2, :] == 0).astype(jnp.float32)
    named = jnp.broadcast_to(first + second, (T, T)).T
    row = lax.broadcasted_iota(jnp.int32, (T, T), 0)
    col = lax.broadcasted_iota(jnp.int32, (T, T), 1)
    below = jnp.where(col < row, 1.0, 0.0).astype(jnp.bfloat16)
    rank = dot_nn(below, named.astype(jnp.bfloat16))
    sel_t = jnp.where((rank == col.astype(jnp.float32)) & (named > 0.5), 1.0, 0.0)
    sel_out_ref[...] = sel_t.astype(jnp.bfloat16)
    sel = sel_t.T
    sel_ref[...] = sel[:CAP].astype(jnp.bfloat16)
    share = share_ref[...]
    coef = jnp.where(first > 0.5, share, 1.0 - share)
    coef_ref[...] = jnp.broadcast_to(
        jnp.sum(sel[:CAP] * coef, axis=1, keepdims=True), coef_ref.shape
    )
    pre_ref[...] = jnp.zeros_like(pre_ref)
    back_ref[...] = jnp.zeros_like(back_ref)

    pl.semaphore_wait(barrier, len(peers))

    def remote(source, target, send, recv, peer):
        return pltpu.make_async_remote_copy(
            src_ref=source,
            dst_ref=target,
            send_sem=send,
            recv_sem=recv,
            device_id=peer,
            device_id_type=MESH,
        )

    def block(b_, a_, count=1):
        return pl.ds(pl.multiple_of(((c * B + b_) * A + a_) * CAP, CAP), count * CAP)

    def passed(p, rows, slot, peer):
        ref = buf.at[p, rows]
        return remote(ref, ref, g_send.at[p, slot], g_recv.at[p, slot], peer)

    def g_diag(p):
        return passed(p, block(b, a), 0, diag)

    def g_mate(p):
        return passed(p, block(b, a), 1, mate)

    def g_cross(p):
        return passed(p, block(b, a_diag), 2, mate)

    def g_sib(p, j):
        return passed(p, block(lax.rem(b + j, B), 0, A), 3 + j, sibling)

    def g_x_own(p, j):
        return passed(p, block(b, a), 3 + B + 3 * j, x_peers[j])

    def g_x_pair(p, j):
        return passed(p, block(b, a_pair, 2), 4 + B + 3 * j, x_peers[j])

    def g_x_mate(p, j):
        return passed(p, block(b, a_mate), 5 + B + 3 * j, x_peers[j])

    def g_turn(p, j):
        return passed(p, block(lax.rem(b + B - 1 - j, B), a), 5 + B + 3 * j, mate)

    key_rows = local_ref.shape[0] // KEY_PIECES

    def ys(p):
        rows = pl.ds(pl.multiple_of(p * key_rows, 8), key_rows)
        copies = []
        for j in range(R - 1):
            copies.append(
                remote(local_ref.at[rows], local_all.at[r, rows], y_send.at[p, j, 0], y_recv.at[p, j, 0], y_peers[j])
            )
            copies.append(
                remote(mom_ref.at[rows], mom_all.at[r, rows], y_send.at[p, j, 1], y_recv.at[p, j, 1], y_peers[j])
            )
        return copies

    def even(p, then, otherwise):
        pl.when(lax.rem(p, 2) == 0)(then)
        pl.when(lax.rem(p, 2) == 1)(otherwise)

    def pick(p):
        pltpu.make_async_copy(tok_ref.at[:, pl.ds(0, width)], src.at[p], src_sem.at[p]).wait()
        buf[p, block(b, a), :] = dot_nn(sel_ref[...], src[p]).astype(jnp.bfloat16)
        g_diag(p).start()
        for j in range(B - 1):
            g_x_own(p, j).start()
        g_mate(p).start()

        @pl.when(p < KEY_PIECES)
        def _():
            for copy in ys(p):
                copy.start()

    def second_round(p):
        g_diag(p).wait_recv()
        g_cross(p).start()
        g_mate(p).wait_recv()

        @pl.when(lax.rem(p, 2) == 0)
        def _():
            for j in range(B - 1):
                g_x_mate(p, j).start()

    def across(p):
        g_cross(p).wait_recv()
        for j in range(B - 1):
            g_x_pair(p, j).start()
        for j in range(B - 1):
            g_x_own(p, j).wait_recv()

        @pl.when(lax.rem(p, 2) == 1)
        def _():
            for j in range(B - 1):
                g_turn(p, j).start()

        g_sib(p, 0).start()

    def aside(p):
        def by_x():
            for j in range(B - 1):
                g_x_mate(p, j).wait_recv()

        def by_mate():
            for j in range(B - 1):
                g_turn(p, j).wait_recv()

        for j in range(B - 1):
            g_x_pair(p, j).wait_recv()
        even(p, by_x, by_mate)
        for j in range(1, B):
            g_sib(p, j).start()

    def multiply(p):
        for j in range(B):
            g_sib(p, j).wait_recv()

        @pl.when(p < K)
        def _():
            rows = pl.ds(pl.multiple_of(p * width, width), width)
            pltpu.make_async_copy(up_ref.at[pl.ds(0, width)], upv.at[rows], up_sem.at[p]).wait()
            pre_ref[...] += dot_nn(buf[p], upv[rows, :])

        @pl.when(p >= K)
        def _():
            k = p - K
            pltpu.make_async_copy(
                down_ref.at[:, pl.ds(0, width)], downv.at[k], down_sem.at[k]
            ).wait()
            back_ref[...] += dot_nt(buf[p], downv[k])

    staged(NP, [(0, pick), (2, second_round), (3, across), (5, aside), (6, multiply)])

    pre = pre_ref[...]
    sig = jax.nn.sigmoid(pre)
    hid_ref[...] = (back_ref[...] * sig * (1.0 + pre * (1.0 - sig))).astype(jnp.bfloat16)

    wide = part.shape[-1]
    other_half = pl.ds(pl.multiple_of((1 - c) * half, half), half)

    def inner(a_, count=1):
        return pl.ds(pl.multiple_of(a_ * CAP, CAP), count * CAP)

    def back(source, target, q, slot, peer):
        return remote(source, target, r_send.at[q, slot], r_recv.at[q, slot], peer)

    def r_sib(q):
        return back(sib_out.at[q], sib_in.at[q], q, 0, sibling)

    def r_mate(q):
        return back(m_out.at[q], m_in.at[q], q, 1, mate)

    def r_diag(q):
        return back(d_out.at[q], d_in.at[q], q, 2, diag)

    def r_x_all(q, j):
        return back(x_out.at[q, j], x_in.at[q, j], q, 3 + 3 * j, x_peers[j])

    def r_x_pair(q, j):
        rows = inner(a_pair, 2)
        return back(x_out.at[q, j, rows], x_in.at[q, j, rows], q, 3 + 3 * j, x_peers[j])

    def r_x_own(q, j):
        rows = inner(a)
        return back(x_out.at[q, j, rows], x_in.at[q, j, rows], q, 4 + 3 * j, x_peers[j])

    def r_turn(q, j):
        return back(n_out.at[q, j], n_in.at[q, j], q, 5 + 3 * j, mate)

    def produce(q):
        rows = pl.ds(pl.multiple_of(q * wide, wide), wide)
        part[q] = dot_nt(hid_ref[...], upv[rows, :])
        sib_out[q] = part[q, other_half, :].astype(jnp.bfloat16)
        r_sib(q).start()

    def pair(q):
        r_sib(q).wait_recv()
        for j in range(B - 1):
            b_ = lax.rem(b + j + 1, B)
            there = pl.ds(pl.multiple_of(b_ * column, column), column)
            mine = block(b_, 0, A)
            total = part[q, mine, :] + sib_in[q, there, :].astype(jnp.float32)
            part[q, mine, :] = total

            def whole():
                x_out[q, j] = part[q, mine, :].astype(jnp.bfloat16)
                r_x_all(q, j).start()

            def split():
                n_out[q, j] = part[q, block(b_, a_mate), :].astype(jnp.bfloat16)
                r_turn(q, j).start()
                x_out[q, j, inner(a_pair, 2), :] = part[q, block(b_, a_pair, 2), :].astype(
                    jnp.bfloat16
                )
                r_x_pair(q, j).start()

            even(q, whole, split)
        here = pl.ds(pl.multiple_of(b * column, column), column)
        mine = block(b, 0, A)
        part[q, mine, :] = part[q, mine, :] + sib_in[q, here, :].astype(jnp.float32)

    def turned(q):
        @pl.when(lax.rem(q, 2) == 1)
        def _():
            for j in range(B - 1):
                b_ = lax.rem(b + j + 1, B)
                r_turn(q, j).wait_recv()
                x_out[q, j, inner(a), :] = (
                    part[q, block(b_, a), :] + n_in[q, j].astype(jnp.float32)
                ).astype(jnp.bfloat16)
                r_x_own(q, j).start()

    def chain(q):
        def whole():
            mine = block(b, 0, A)
            for j in range(B - 1):
                r_x_all(q, j).wait_recv()
                part[q, mine, :] = part[q, mine, :] + x_in[q, j].astype(jnp.float32)

        def split():
            for j in range(B - 1):
                r_x_pair(q, j).wait_recv()
                r_x_own(q, j).wait_recv()
                for b_, rows in ((block(b, a_pair, 2), inner(a_pair, 2)), (block(b, a), inner(a))):
                    part[q, b_, :] = part[q, b_, :] + x_in[q, j, rows, :].astype(jnp.float32)

        even(q, whole, split)
        m_out[q, 0] = part[q, block(b, a_mate), :].astype(jnp.bfloat16)
        m_out[q, 1] = part[q, block(b, a_cross), :].astype(jnp.bfloat16)
        r_mate(q).start()

    def far(q):
        r_mate(q).wait_recv()
        d_out[q] = (part[q, block(b, a_diag), :] + m_in[q, 1].astype(jnp.float32)).astype(
            jnp.bfloat16
        )
        r_diag(q).start()

    def finish(q):
        r_diag(q).wait_recv()
        total = part[q, block(b, a), :] + m_in[q, 0].astype(jnp.float32)
        total = total + d_in[q].astype(jnp.float32)
        cols = pl.ds(pl.multiple_of(q * wide, 128), wide)
        res_ref[:, cols] = (coef_ref[:, 0:1] * total).astype(jnp.bfloat16)

    staged(KR, [(0, produce), (1, pair), (2, turned), (4, chain), (5, far), (6, finish)])

    def sent_gather(p, carry):
        copies = [g_diag(p), g_mate(p), g_cross(p)]
        for j in range(B):
            copies.append(g_sib(p, j))
        for j in range(B - 1):
            copies += [g_x_own(p, j), g_x_pair(p, j), g_x_mate(p, j)]
        for copy in copies:
            copy.wait_send()
        return carry

    def sent_reduce(q, carry):
        for copy in (r_sib(q), r_mate(q), r_diag(q)):
            copy.wait_send()

        def whole():
            for j in range(B - 1):
                r_x_all(q, j).wait_send()

        def split():
            for j in range(B - 1):
                for copy in (r_x_pair(q, j), r_x_own(q, j), r_turn(q, j)):
                    copy.wait_send()

        even(q, whole, split)
        return carry

    def keys_done(p, carry):
        for copy in ys(p):
            copy.wait()
        return carry

    lax.fori_loop(0, NP, sent_gather, 0)
    lax.fori_loop(0, KR, sent_reduce, 0)
    lax.fori_loop(0, KEY_PIECES, keys_done, 0)
    own_local.wait()
    own_mom.wait()


def exchange(R, F, ids, share, tokens, grads, up, down, local, momentum):
    A = MAJOR
    B = F // (2 * A)
    K = PIECES
    KR = BACK_PIECES
    T, D = tokens.shape
    H = up.shape[1]
    width = D // K
    wide = D // KR
    rows = F * CAP
    column = A * CAP
    half = B * column
    dma = pltpu.SemaphoreType.DMA
    vmem = pl.BlockSpec(memory_space=pltpu.VMEM)
    hbm = pl.BlockSpec(memory_space=pl.ANY)
    return pl.pallas_call(
        functools.partial(kernel, R, B, K, KR),
        out_shape=(
            jax.ShapeDtypeStruct((CAP, D), jnp.bfloat16),
            jax.ShapeDtypeStruct((T, T), jnp.bfloat16),
            jax.ShapeDtypeStruct((R,) + local.shape, jnp.float32),
            jax.ShapeDtypeStruct((R,) + momentum.shape, jnp.float32),
        ),
        in_specs=[vmem, vmem, hbm, hbm, hbm, hbm, hbm, hbm],
        out_specs=(vmem, vmem, hbm, hbm),
        scratch_shapes=[
            pltpu.VMEM((2 * K, T, width), jnp.bfloat16),
            pltpu.VMEM((2 * K, rows, width), jnp.bfloat16),
            pltpu.VMEM((D, H), jnp.bfloat16),
            pltpu.VMEM((K, H, width), jnp.bfloat16),
            pltpu.VMEM((CAP, T), jnp.bfloat16),
            pltpu.VMEM((CAP, 128), jnp.float32),
            pltpu.VMEM((rows, H), jnp.float32),
            pltpu.VMEM((rows, H), jnp.float32),
            pltpu.VMEM((rows, H), jnp.bfloat16),
            pltpu.VMEM((KR, rows, wide), jnp.float32),
            pltpu.VMEM((KR, half, wide), jnp.bfloat16),
            pltpu.VMEM((KR, half, wide), jnp.bfloat16),
            pltpu.VMEM((KR, B - 1, column, wide), jnp.bfloat16),
            pltpu.VMEM((KR, B - 1, column, wide), jnp.bfloat16),
            pltpu.VMEM((KR, B - 1, CAP, wide), jnp.bfloat16),
            pltpu.VMEM((KR, B - 1, CAP, wide), jnp.bfloat16),
            pltpu.VMEM((KR, 2, CAP, wide), jnp.bfloat16),
            pltpu.VMEM((KR, 2, CAP, wide), jnp.bfloat16),
            pltpu.VMEM((KR, CAP, wide), jnp.bfloat16),
            pltpu.VMEM((KR, CAP, wide), jnp.bfloat16),
            dma((2 * K,)),
            dma((K,)),
            dma((K,)),
            dma((2,)),
            dma((KEY_PIECES, R - 1, 2)),
            dma((KEY_PIECES, R - 1, 2)),
            dma((2 * K, 4 * B)),
            dma((2 * K, 4 * B)),
            dma((KR, 3 * B)),
            dma((KR, 3 * B)),
        ],
        compiler_params=pltpu.CompilerParams(
            collective_id=0, has_side_effects=True, vmem_limit_bytes=60 * 1024 * 1024
        ),
        cost_estimate=pl.CostEstimate(
            flops=6 * rows * D * H, bytes_accessed=8 * D * H, transcendentals=rows * H
        ),
    )(ids, share, tokens, grads, up, down, local, momentum)


def tail_kernel(
    R, sel_ref, res_ref, outer_ref, local_ref, mom_ref, grad_ref, new_ref, moved_ref, copy_ref
):
    r = lax.axis_index("replica")
    width = mom_ref.shape[-1]
    grad_ref[...] = dot_nn(sel_ref[:, :CAP], res_ref[...]).astype(jnp.bfloat16)
    for one in range(R):
        cols = slice(one * width, (one + 1) * width)
        outer = outer_ref[:, cols]
        pseudo = outer - local_ref[0, :, cols]
        for other in range(1, R):
            pseudo = pseudo + (outer - local_ref[other, :, cols])
        pseudo = pseudo / R
        moved = outer_beta * mom_ref[one] + pseudo
        new_outer = outer - outer_rate * (pseudo + outer_beta * moved)
        new_ref[:, cols] = new_outer
        copy_ref[:, cols] = new_outer.astype(jnp.bfloat16)

        @pl.when(r == one)
        def _():
            moved_ref[...] = moved


def tail(R, sel, result, outer, local_all, mom_all):
    T = sel.shape[0]
    D = result.shape[1]
    rows, keys = outer.shape
    width = mom_all.shape[2]
    G = TAIL_STEPS
    few, cols = rows // G, D // G
    return pl.pallas_call(
        functools.partial(tail_kernel, R),
        grid=(G,),
        out_shape=(
            jax.ShapeDtypeStruct((T, D), jnp.bfloat16),
            jax.ShapeDtypeStruct((rows, keys), jnp.float32),
            jax.ShapeDtypeStruct((rows, width), jnp.float32),
            jax.ShapeDtypeStruct((rows, keys), jnp.bfloat16),
        ),
        in_specs=[
            pl.BlockSpec((T, T), lambda g: (0, 0)),
            pl.BlockSpec((CAP, cols), lambda g: (0, g)),
            pl.BlockSpec((few, keys), lambda g: (g, 0)),
            pl.BlockSpec((R, few, keys), lambda g: (0, g, 0)),
            pl.BlockSpec((R, few, width), lambda g: (0, g, 0)),
        ],
        out_specs=(
            pl.BlockSpec((T, cols), lambda g: (0, g)),
            pl.BlockSpec((few, keys), lambda g: (g, 0)),
            pl.BlockSpec((few, width), lambda g: (g, 0)),
            pl.BlockSpec((few, keys), lambda g: (g, 0)),
        ),
        compiler_params=pltpu.CompilerParams(vmem_limit_bytes=32 * 1024 * 1024),
    )(sel, result, outer, local_all, mom_all)


def per_device(
    R,
    F,
    tokens,
    grad_out,
    expert_ids,
    gate_share,
    up_weight,
    down_weight,
    local_keys,
    outer_keys,
    momentum,
):
    result, sel, local_all, mom_all = exchange(
        R,
        F,
        expert_ids[0].T,
        gate_share,
        tokens[0],
        grad_out[0],
        up_weight[0],
        down_weight[0],
        local_keys[0],
        momentum,
    )
    input_grad, new_outer, new_momentum, outer_copy = tail(
        R, sel, result, outer_keys, local_all, mom_all
    )
    return (input_grad[None], new_outer, new_momentum, outer_copy)


def solution(mesh):
    placed = (
        P("replica", "fsdp", None),
        P("replica", "fsdp", None),
        P("replica", "fsdp", None),
        P("replica", "fsdp"),
        P("replica", None, "fsdp"),
        P("replica", "fsdp", None),
        P("replica", "fsdp", None),
        P("fsdp", None),
        P("fsdp", "replica"),
    )
    return jax.shard_map(
        functools.partial(per_device, mesh.shape["replica"], mesh.shape["fsdp"]),
        mesh=mesh,
        in_specs=placed,
        out_specs=(
            P("replica", "fsdp", None),
            P("fsdp", None),
            P("fsdp", "replica"),
            P("fsdp", None),
        ),
        check_vma=False,
    )
```

time: 84.7 us -> 96 us (1.13)
  Pallas kernels: 77 us -> 90.8 us
  matrix products: 1.69 us -> 0 us
  other arithmetic: 1.36 us -> 0 us
    pallas_call x1 -> x2, Pallas kernels: 77 us -> 90.8 us  [the longest x1 88 us: exchange(): pl.pallas_call(functools.partial(kernel, R, B, K, KR), out_shape=(jax.Sha...]
    unnamed x9 -> x10, local copies, waits for them, and re-layouts: 1.76 us -> 4.22 us
    dot_general x1 -> x0, matrix products: 1.69 us -> none  [per_device(): jnp.dot(sel[:, :CAP], result, preferred_element_type=jnp.float32)]
    convert_element_type x1 -> x0, other arithmetic: 1.36 us -> none  [per_device(): new_outer.astype(jnp.bfloat16)]
    squeeze x1 -> x0, local copies, waits for them, and re-layouts: 1.28 us -> none  [per_device(): every = jnp.concatenate([mom_all[one] for one in range(R)], axis=1)]
where the time goes in v2:
time: 96 us; the launch traced here: 95.7 us
  Pallas kernels  90.8 us (95%)
  local copies, waits for them, and re-layouts  4.22 us (4%)
    pallas_call x1, Pallas kernels, exchange(): pl.pallas_call(functools.partial(kernel, R, B, K, KR), out_shape=(jax.Sha...  88 us
    unnamed x10, local copies, waits for them, and re-layouts  4.22 us
    pallas_call x1, Pallas kernels, tail(): pl.pallas_call(functools.partial(tail_kernel, R), grid=(G,), out_shape=(j...  2.89 us

profile of v2, /device:TPU:0, one launch (start us, length us, event | category | flops | bytes accessed | tf_op | source)
XLA Modules:
  0.0 95.7 jit_solution(18356288170643449976)
XLA Ops:
  0.6 0.0 copy-start.1
  0.6 88.0 %shard_map.120 = (bf16[16,6144]{1,0:T(8,128)(2,1)}, bf16[128,128]{1,0:T(8,128)(2,1)}, f32[2,384,512]{2,1,0:T(8,128)}, f32[2,384,256]{2,1,0:T(8,128)}) custom-call(s32[2,128]{1,0:T(2,128)} %bitcast.15, f32[1,128]{1,0:T(1,128)} %share_ref.1, bf16[128,6144]{1,0:T(8,128)(2,1)} %bitcast.11, bf16[128,6144]{1,0:T(8,128)(2,1)} %bitcast.12, ...), custom_call_target="tpu_custom_call" | custom-call | flops 4831838208 | bytes 25165824 | tf_op jit(solution)/shard_map/pallas_call | solution.py:461
  88.6 0.0 copy-done.1
  88.6 0.0 copy-start
  88.6 1.4 %copy-done = f32[2,384,512]{2,1,0:T(8,128)S(1)} copy-done((f32[2,384,512]{2,1,0:T(8,128)S(1)}, f32[2,384,512]{2,1,0:T(8,128)}, u32[]{:S(2)}) %copy-start) | copy-done | bytes 1572888
  90.0 0.0 copy-start.2
  90.0 1.1 %copy-done.2 = f32[2,384,256]{2,1,0:T(8,128)S(1)} copy-done((f32[2,384,256]{2,1,0:T(8,128)S(1)}, f32[2,384,256]{2,1,0:T(8,128)}, u32[]{:S(2)}) %copy-start.2) | copy-done | bytes 786456
  91.2 0.0 copy-start.3
  91.2 0.9 copy-done.3
  92.1 0.0 copy-start.4
  92.1 0.8 copy-done.4
  92.8 2.9 %shard_map.121 = (bf16[128,6144]{1,0:T(8,128)(2,1)}, f32[384,512]{1,0:T(8,128)}, f32[384,256]{1,0:T(8,128)}, bf16[384,512]{1,0:T(8,128)(2,1)}) custom-call(bf16[128,128]{1,0:T(8,128)(2,1)S(1)} %copy-done.4, bf16[16,6144]{1,0:T(8,128)(2,1)S(1)} %copy-done.3, f32[384,512]{1,0:T(8,128)S(1)} %copy-done.1, f32[2,384,512]{2,1,0:T(8,128)S(1)} %copy-done, ...), custom_call_target="tpu_custom_call" | custom-call | tf_op jit(solution)/shard_map/pallas_call | solution.py:542
Async XLA Ops:
  0.6 88.0 %copy-start.1 = (f32[384,512]{1,0:T(8,128)S(1)}, f32[384,512]{1,0:T(8,128)}, u32[]{:S(2)}) copy-start(f32[384,512]{1,0:T(8,128)} %outer_ref.1) | copy-start | bytes 2359300
  88.6 1.4 %copy-start = (f32[2,384,512]{2,1,0:T(8,128)S(1)}, f32[2,384,512]{2,1,0:T(8,128)}, u32[]{:S(2)}) copy-start(f32[2,384,512]{2,1,0:T(8,128)} %get-tuple-element.14.local_ref) | copy-start | bytes 4718596
  90.0 1.1 %copy-start.2 = (f32[2,384,256]{2,1,0:T(8,128)S(1)}, f32[2,384,256]{2,1,0:T(8,128)}, u32[]{:S(2)}) copy-start(f32[2,384,256]{2,1,0:T(8,128)} %get-tuple-element.15.mom_ref) | copy-start | bytes 2359300
  91.2 0.9 copy-start.3
  92.1 0.8 copy-start.4

commit v3 on v1

--- a/solution.py
+++ b/solution.py
@@ -9,8 +9,10 @@
 
 CAP = 16
 MAJOR = 4
-PIECES = 8
-KEY_PIECES = 8
+PIECES = 6
+BACK_PIECES = 8
+KEY_PIECES = 4
+TAIL_STEPS = 4
 
 outer_beta = 0.9
 outer_rate = 0.7
@@ -47,6 +49,7 @@
     A,
     B,
     K,
+    KR,
     ids_ref,
     share_ref,
     tok_ref,
@@ -117,7 +120,7 @@
         pltpu.make_async_copy(tok_ref.at[:, cols], src.at[k], src_sem.at[k]).start()
     for k in range(K):
         cols = pl.ds(k * width, width)
-        pltpu.make_async_copy(up_ref.at[cols], upv.at[k], up_sem.at[k]).start()
+        pltpu.make_async_copy(up_ref.at[cols], upv.at[cols], up_sem.at[k]).start()
     for k in range(K):
         cols = pl.ds(k * width, width)
         pltpu.make_async_copy(grad_ref.at[:, cols], src.at[K + k], src_sem.at[K + k]).start()
@@ -134,11 +137,10 @@
     for peer in peers:
         pl.semaphore_signal(barrier, inc=1, device_id=peer, device_id_type=MESH)
 
-    T = ids_ref.shape[0]
-    ids = ids_ref[...]
-    first = (ids[:, 0:1] == 0).astype(jnp.float32)
-    second = (ids[:, 1:2] == 0).astype(jnp.float32)
-    named = jnp.broadcast_to(first + second, (T, T))
+    T = ids_ref.shape[1]
+    first = (ids_ref[0:1, :] == 0).astype(jnp.float32)
+    second = (ids_ref[1:2, :] == 0).astype(jnp.float32)
+    named = jnp.broadcast_to(first + second, (T, T)).T
     row = lax.broadcasted_iota(jnp.int32, (T, T), 0)
     col = lax.broadcasted_iota(jnp.int32, (T, T), 1)
     below = jnp.where(col < row, 1.0, 0.0).astype(jnp.bfloat16)
@@ -147,9 +149,8 @@
     sel_out_ref[...] = sel_t.astype(jnp.bfloat16)
     sel = sel_t.T
     sel_ref[...] = sel[:CAP].astype(jnp.bfloat16)
-    first_row = jnp.broadcast_to(first, (T, T)).T
     share = share_ref[...]
-    coef = jnp.where(first_row[:CAP] > 0.5, share, 1.0 - share)
+    coef = jnp.where(first > 0.5, share, 1.0 - share)
     coef_ref[...] = jnp.broadcast_to(
         jnp.sum(sel[:CAP] * coef, axis=1, keepdims=True), coef_ref.shape
     )
@@ -233,8 +234,9 @@
 
         @pl.when(p < K)
         def _():
-            pltpu.make_async_copy(up_ref.at[pl.ds(0, width)], upv.at[p], up_sem.at[p]).wait()
-            pre_ref[...] += dot_nn(buf[p], upv[p])
+            rows = pl.ds(pl.multiple_of(p * width, width), width)
+            pltpu.make_async_copy(up_ref.at[pl.ds(0, width)], upv.at[rows], up_sem.at[p]).wait()
+            pre_ref[...] += dot_nn(buf[p], upv[rows, :])
 
         @pl.when(p >= K)
         def _():
@@ -244,12 +246,17 @@
             ).wait()
             back_ref[...] += dot_nt(buf[p], downv[k])
 
-    staged(NP, [(0, pick), (2, across), (4, aside), (5, multiply)])
+    def sent(p):
+        for copy in gz(p) + gx(p) + [gs(p, j) for j in range(B)]:
+            copy.wait_send()
+
+    staged(NP, [(0, pick), (3, across), (5, aside), (6, multiply), (6, sent)])
 
     pre = pre_ref[...]
     sig = jax.nn.sigmoid(pre)
     hid_ref[...] = (back_ref[...] * sig * (1.0 + pre * (1.0 - sig))).astype(jnp.bfloat16)
 
+    wide = part.shape[-1]
     own_half = pl.ds(pl.multiple_of(c * half, half), half)
     other_half = pl.ds(pl.multiple_of((1 - c) * half, half), half)
 
@@ -269,7 +276,8 @@
         ]
 
     def produce(q):
-        part[q] = dot_nt(hid_ref[...], upv[q])
+        rows = pl.ds(pl.multiple_of(q * wide, wide), wide)
+        part[q] = dot_nt(hid_ref[...], upv[rows, :])
         sib_out[q] = part[q, other_half, :].astype(jnp.bfloat16)
         rs(q).start()
 
@@ -302,28 +310,20 @@
         for j, copy in enumerate(rz(q)):
             copy.wait_recv()
             total = total + z_in[q, j].astype(jnp.float32)
-        cols = pl.ds(pl.multiple_of(q * width, 128), width)
+        cols = pl.ds(pl.multiple_of(q * wide, 128), wide)
         res_ref[:, cols] = (coef_ref[:, 0:1] * total).astype(jnp.bfloat16)
 
-    staged(K, [(0, produce), (1, pair), (3, chain), (5, finish)])
-
-    def sent_gather(p, carry):
-        for copy in gz(p) + gx(p) + [gs(p, j) for j in range(B)]:
-            copy.wait_send()
-        return carry
-
-    def sent_reduce(q, carry):
+    def returned(q):
         for copy in [rs(q)] + rx(q) + rz(q):
             copy.wait_send()
-        return carry
+
+    staged(KR, [(0, produce), (1, pair), (3, chain), (5, finish), (5, returned)])
 
     def keys_done(p, carry):
         for copy in ys(p):
             copy.wait()
         return carry
 
-    lax.fori_loop(0, NP, sent_gather, 0)
-    lax.fori_loop(0, K, sent_reduce, 0)
     lax.fori_loop(0, KEY_PIECES, keys_done, 0)
     own_local.wait()
     own_mom.wait()
@@ -333,10 +333,12 @@
     A = MAJOR
     B = F // (2 * A)
     K = PIECES
+    KR = BACK_PIECES
     D = tokens.shape[1]
     H = up.shape[1]
     T = tokens.shape[0]
     width = D // K
+    wide = D // KR
     rows = F * CAP
     column = A * CAP
     half = B * column
@@ -344,7 +346,7 @@
     vmem = pl.BlockSpec(memory_space=pltpu.VMEM)
     hbm = pl.BlockSpec(memory_space=pl.ANY)
     return pl.pallas_call(
-        functools.partial(kernel, R, A, B, K),
+        functools.partial(kernel, R, A, B, K, KR),
         out_shape=(
             jax.ShapeDtypeStruct((CAP, D), jnp.bfloat16),
             jax.ShapeDtypeStruct((T, T), jnp.bfloat16),
@@ -356,20 +358,20 @@
         scratch_shapes=[
             pltpu.VMEM((2 * K, T, width), jnp.bfloat16),
             pltpu.VMEM((2 * K, rows, width), jnp.bfloat16),
-            pltpu.VMEM((K, width, H), jnp.bfloat16),
+            pltpu.VMEM((D, H), jnp.bfloat16),
             pltpu.VMEM((K, H, width), jnp.bfloat16),
             pltpu.VMEM((CAP, T), jnp.bfloat16),
             pltpu.VMEM((CAP, 128), jnp.float32),
             pltpu.VMEM((rows, H), jnp.float32),
             pltpu.VMEM((rows, H), jnp.float32),
             pltpu.VMEM((rows, H), jnp.bfloat16),
-            pltpu.VMEM((K, rows, width), jnp.float32),
-            pltpu.VMEM((K, half, width), jnp.bfloat16),
-            pltpu.VMEM((K, half, width), jnp.bfloat16),
-            pltpu.VMEM((K, B - 1, column, width), jnp.bfloat16),
-            pltpu.VMEM((K, B - 1, column, width), jnp.bfloat16),
-            pltpu.VMEM((K, A - 1, CAP, width), jnp.bfloat16),
-            pltpu.VMEM((K, A - 1, CAP, width), jnp.bfloat16),
+            pltpu.VMEM((KR, rows, wide), jnp.float32),
+            pltpu.VMEM((KR, half, wide), jnp.bfloat16),
+            pltpu.VMEM((KR, half, wide), jnp.bfloat16),
+            pltpu.VMEM((KR, B - 1, column, wide), jnp.bfloat16),
+            pltpu.VMEM((KR, B - 1, column, wide), jnp.bfloat16),
+            pltpu.VMEM((KR, A - 1, CAP, wide), jnp.bfloat16),
+            pltpu.VMEM((KR, A - 1, CAP, wide), jnp.bfloat16),
             dma((2 * K,)),
             dma((K,)),
             dma((K,)),
@@ -382,12 +384,12 @@
             dma((2 * K, B - 1)),
             dma((2 * K, B)),
             dma((2 * K, B)),
-            dma((K,)),
-            dma((K,)),
-            dma((K, B - 1)),
-            dma((K, B - 1)),
-            dma((K, A - 1)),
-            dma((K, A - 1)),
+            dma((KR,)),
+            dma((KR,)),
+            dma((KR, B - 1)),
+            dma((KR, B - 1)),
+            dma((KR, A - 1)),
+            dma((KR, A - 1)),
         ],
         compiler_params=pltpu.CompilerParams(
             collective_id=0, has_side_effects=True, vmem_limit_bytes=60 * 1024 * 1024
@@ -396,6 +398,62 @@
             flops=6 * rows * D * H, bytes_accessed=8 * D * H, transcendentals=rows * H
         ),
     )(ids, share, tokens, grads, up, down, local, momentum)
+
+
+def tail_kernel(
+    R, sel_ref, res_ref, outer_ref, local_ref, mom_ref, grad_ref, new_ref, moved_ref, copy_ref
+):
+    r = lax.axis_index("replica")
+    width = mom_ref.shape[-1]
+    grad_ref[...] = dot_nn(sel_ref[:, :CAP], res_ref[...]).astype(jnp.bfloat16)
+    for one in range(R):
+        cols = slice(one * width, (one + 1) * width)
+        outer = outer_ref[:, cols]
+        pseudo = outer - local_ref[0, :, cols]
+        for other in range(1, R):
+            pseudo = pseudo + (outer - local_ref[other, :, cols])
+        pseudo = pseudo / R
+        moved = outer_beta * mom_ref[one] + pseudo
+        new_outer = outer - outer_rate * (pseudo + outer_beta * moved)
+        new_ref[:, cols] = new_outer
+        copy_ref[:, cols] = new_outer.astype(jnp.bfloat16)
+
+        @pl.when(r == one)
+        def _():
+            moved_ref[...] = moved
+
+
+def tail(R, sel, result, outer, local_all, mom_all):
+    T = sel.shape[0]
+    D = result.shape[1]
+    rows, keys = outer.shape
+    width = mom_all.shape[2]
+    G = TAIL_STEPS
+    few, cols = rows // G, D // G
+    return pl.pallas_call(
+        functools.partial(tail_kernel, R),
+        grid=(G,),
+        out_shape=(
+            jax.ShapeDtypeStruct((T, D), jnp.bfloat16),
+            jax.ShapeDtypeStruct((rows, keys), jnp.float32),
+            jax.ShapeDtypeStruct((rows, width), jnp.float32),
+            jax.ShapeDtypeStruct((rows, keys), jnp.bfloat16),
+        ),
+        in_specs=[
+            pl.BlockSpec((T, T), lambda g: (0, 0)),
+            pl.BlockSpec((CAP, cols), lambda g: (0, g)),
+            pl.BlockSpec((few, keys), lambda g: (g, 0)),
+            pl.BlockSpec((R, few, keys), lambda g: (0, g, 0)),
+            pl.BlockSpec((R, few, width), lambda g: (0, g, 0)),
+        ],
+        out_specs=(
+            pl.BlockSpec((T, cols), lambda g: (0, g)),
+            pl.BlockSpec((few, keys), lambda g: (g, 0)),
+            pl.BlockSpec((few, width), lambda g: (g, 0)),
+            pl.BlockSpec((few, keys), lambda g: (g, 0)),
+        ),
+        compiler_params=pltpu.CompilerParams(vmem_limit_bytes=60 * 1024 * 1024),
+    )(sel, result, outer, local_all, mom_all)
 
 
 def per_device(
@@ -414,7 +472,7 @@
     result, sel, local_all, mom_all = exchange(
         R,
         F,
-        expert_ids[0],
+        expert_ids[0].T,
         gate_share,
         tokens[0],
         grad_out[0],
@@ -423,19 +481,10 @@
         local_keys[0],
         momentum,
     )
-    input_grad = jnp.dot(
-        sel[:, :CAP], result, preferred_element_type=jnp.float32
-    ).astype(jnp.bfloat16)
-    pseudo = outer_keys - local_all[0]
-    for one in range(1, R):
-        pseudo = pseudo + (outer_keys - local_all[one])
-    pseudo = pseudo / R
-    every = jnp.concatenate([mom_all[one] for one in range(R)], axis=1)
-    moved = outer_beta * every + pseudo
-    new_outer = outer_keys - outer_rate * (pseudo + outer_beta * moved)
-    width = momentum.shape[1]
-    new_momentum = lax.dynamic_slice_in_dim(moved, lax.axis_index("replica") * width, width, 1)
-    return (input_grad[None], new_outer, new_momentum, new_outer.astype(jnp.bfloat16))
+    input_grad, new_outer, new_momentum, outer_copy = tail(
+        R, sel, result, outer_keys, local_all, mom_all
+    )
+    return (input_grad[None], new_outer, new_momentum, outer_copy)
 
 
 def solution(mesh):

time: 84.7 us -> 84.2 us (level)
  Pallas kernels: 77 us -> 83.4 us
  local copies, waits for them, and re-layouts: 3.82 us -> 0 us
  matrix products: 1.69 us -> 0 us
  other arithmetic: 1.36 us -> 0 us
    pallas_call x1 -> x2, Pallas kernels: 77 us -> 83.4 us  [the longest x1 78.6 us: exchange(): pl.pallas_call(functools.partial(kernel, R, A, B, K, KR), out_shape=(jax....]
    unnamed x9 -> x0, local copies, waits for them, and re-layouts: 1.76 us -> none
    dot_general x1 -> x0, matrix products: 1.69 us -> none  [per_device(): jnp.dot(sel[:, :CAP], result, preferred_element_type=jnp.float32)]
    convert_element_type x1 -> x0, other arithmetic: 1.36 us -> none  [per_device(): new_outer.astype(jnp.bfloat16)]
    squeeze x1 -> x0, local copies, waits for them, and re-layouts: 1.28 us -> none  [per_device(): every = jnp.concatenate([mom_all[one] for one in range(R)], axis=1)]
where the time goes in v3:
time: 84.2 us; the launch traced here: 84 us
  Pallas kernels  83.4 us (99%)
    pallas_call x1, Pallas kernels, exchange(): pl.pallas_call(functools.partial(kernel, R, A, B, K, KR), out_shape=(jax....  78.6 us
    pallas_call x1, Pallas kernels, tail(): pl.pallas_call(functools.partial(tail_kernel, R), grid=(G,), out_shape=(j...  4.8 us

profile of v3, /device:TPU:0, one launch (start us, length us, event | category | flops | bytes accessed | tf_op | source)
XLA Modules:
  0.0 84.0 jit_solution(500571484975254925)
XLA Ops:
  0.6 78.6 %shard_map.120 = (bf16[16,6144]{1,0:T(8,128)(2,1)}, bf16[128,128]{1,0:T(8,128)(2,1)}, f32[2,384,512]{2,1,0:T(8,128)}, f32[2,384,256]{2,1,0:T(8,128)}) custom-call(s32[2,128]{1,0:T(2,128)} %bitcast.15, f32[1,128]{1,0:T(1,128)} %share_ref.1, bf16[128,6144]{1,0:T(8,128)(2,1)} %bitcast.11, bf16[128,6144]{1,0:T(8,128)(2,1)} %bitcast.12, ...), custom_call_target="tpu_custom_call" | custom-call | flops 4831838208 | bytes 25165824 | tf_op jit(solution)/shard_map/pallas_call | solution.py:348
  79.2 4.8 %shard_map.121 = (bf16[128,6144]{1,0:T(8,128)(2,1)}, f32[384,512]{1,0:T(8,128)}, f32[384,256]{1,0:T(8,128)}, bf16[384,512]{1,0:T(8,128)(2,1)}) custom-call(bf16[128,128]{1,0:T(8,128)(2,1)} %get-tuple-element.12.sel_ref, bf16[16,6144]{1,0:T(8,128)(2,1)} %get-tuple-element.13.res_ref, f32[384,512]{1,0:T(8,128)} %outer_ref.1, ...), custom_call_target="tpu_custom_call" | custom-call | tf_op jit(solution)/shard_map/pallas_call | solution.py:433

commit v4 on v3

--- a/solution.py
+++ b/solution.py
@@ -9,10 +9,10 @@
 
 CAP = 16
 MAJOR = 4
-PIECES = 6
+PIECES = 8
 BACK_PIECES = 8
-KEY_PIECES = 4
-TAIL_STEPS = 4
+KEY_ROWS = 24
+TAIL_STEPS = 8
 
 outer_beta = 0.9
 outer_rate = 0.7
@@ -190,10 +190,10 @@
         part_of = buf.at[p, rows_of(lax.rem(b + j, B))]
         return remote(part_of, part_of, gs_send.at[p, j], gs_recv.at[p, j], sibling)
 
-    key_rows = local_ref.shape[0] // KEY_PIECES
+    key_pieces = local_ref.shape[0] // KEY_ROWS
 
     def ys(p):
-        rows = pl.ds(pl.multiple_of(p * key_rows, 8), key_rows)
+        rows = pl.ds(pl.multiple_of(p * KEY_ROWS, 8), KEY_ROWS)
         copies = []
         for j in range(R - 1):
             copies.append(
@@ -211,7 +211,8 @@
         for copy in gz(p):
             copy.start()
 
-        @pl.when(p < KEY_PIECES)
+    def keys(p):
+        @pl.when(p < key_pieces)
         def _():
             for copy in ys(p):
                 copy.start()
@@ -250,7 +251,7 @@
         for copy in gz(p) + gx(p) + [gs(p, j) for j in range(B)]:
             copy.wait_send()
 
-    staged(NP, [(0, pick), (3, across), (5, aside), (6, multiply), (6, sent)])
+    staged(NP, [(0, pick), (4, across), (7, aside), (6, keys), (9, multiply), (10, sent)])
 
     pre = pre_ref[...]
     sig = jax.nn.sigmoid(pre)
@@ -317,14 +318,14 @@
         for copy in [rs(q)] + rx(q) + rz(q):
             copy.wait_send()
 
-    staged(KR, [(0, produce), (1, pair), (3, chain), (5, finish), (5, returned)])
+    staged(KR, [(0, produce), (2, pair), (5, chain), (8, finish), (8, returned)])
 
     def keys_done(p, carry):
         for copy in ys(p):
             copy.wait()
         return carry
 
-    lax.fori_loop(0, KEY_PIECES, keys_done, 0)
+    lax.fori_loop(0, key_pieces, keys_done, 0)
     own_local.wait()
     own_mom.wait()
 
@@ -376,8 +377,8 @@
             dma((K,)),
             dma((K,)),
             dma((2,)),
-            dma((KEY_PIECES, R - 1, 2)),
-            dma((KEY_PIECES, R - 1, 2)),
+            dma((local.shape[0] // KEY_ROWS, R - 1, 2)),
+            dma((local.shape[0] // KEY_ROWS, R - 1, 2)),
             dma((2 * K, A - 1)),
             dma((2 * K, A - 1)),
             dma((2 * K, B - 1)),

time: 84.2 us -> 87.5 us (1.039)
  Pallas kernels: 83.4 us -> 86.6 us
    pallas_call x1, Pallas kernels: 4.8 us -> 7.06 us  [tail(): pl.pallas_call(functools.partial(tail_kernel, R), grid=(G,), out_shape=(j...]
    pallas_call x1, Pallas kernels: 78.6 us -> 79.5 us  [exchange(): pl.pallas_call(functools.partial(kernel, R, A, B, K, KR), out_shape=(jax....]
where the time goes in v4:
time: 87.5 us; the launch traced here: 87.2 us
  Pallas kernels  86.6 us (99%)
    pallas_call x1, Pallas kernels, exchange(): pl.pallas_call(functools.partial(kernel, R, A, B, K, KR), out_shape=(jax....  79.5 us
    pallas_call x1, Pallas kernels, tail(): pl.pallas_call(functools.partial(tail_kernel, R), grid=(G,), out_shape=(j...  7.06 us

profile of v4, /device:TPU:0, one launch (start us, length us, event | category | flops | bytes accessed | tf_op | source)
XLA Modules:
  0.0 87.2 jit_solution(12033441309136224052)
XLA Ops:
  0.6 79.5 %shard_map.120 = (bf16[16,6144]{1,0:T(8,128)(2,1)}, bf16[128,128]{1,0:T(8,128)(2,1)}, f32[2,384,512]{2,1,0:T(8,128)}, f32[2,384,256]{2,1,0:T(8,128)}) custom-call(s32[2,128]{1,0:T(2,128)} %bitcast.15, f32[1,128]{1,0:T(1,128)} %share_ref.1, bf16[128,6144]{1,0:T(8,128)(2,1)} %bitcast.11, bf16[128,6144]{1,0:T(8,128)(2,1)} %bitcast.12, ...), custom_call_target="tpu_custom_call" | custom-call | flops 4831838208 | bytes 25165824 | tf_op jit(solution)/shard_map/pallas_call | solution.py:349
  80.2 7.1 %shard_map.121 = (bf16[128,6144]{1,0:T(8,128)(2,1)}, f32[384,512]{1,0:T(8,128)}, f32[384,256]{1,0:T(8,128)}, bf16[384,512]{1,0:T(8,128)(2,1)}) custom-call(bf16[128,128]{1,0:T(8,128)(2,1)} %get-tuple-element.12.sel_ref, bf16[16,6144]{1,0:T(8,128)(2,1)} %get-tuple-element.13.res_ref, f32[384,512]{1,0:T(8,128)} %outer_ref.1, ...), custom_call_target="tpu_custom_call" | custom-call | tf_op jit(solution)/shard_map/pallas_call | solution.py:434

commit v5 on v4

--- a/solution.py
+++ b/solution.py
@@ -11,8 +11,8 @@
 MAJOR = 4
 PIECES = 8
 BACK_PIECES = 8
-KEY_ROWS = 24
-TAIL_STEPS = 8
+KEY_ROWS = 48
+TAIL_STEPS = 2
 
 outer_beta = 0.9
 outer_rate = 0.7
@@ -86,6 +86,8 @@
     y_recv,
     gz_send,
     gz_recv,
+    go_send,
+    go_recv,
     gx_send,
     gx_recv,
     gs_send,
@@ -172,17 +174,27 @@
     def rows_of(b_):
         return pl.ds(pl.multiple_of((c * B + b_) * column, column), column)
 
+    def place(b_, k):
+        return pl.ds(pl.multiple_of((c * B + b_) * column + k * CAP, CAP), CAP)
+
     def gz(p):
-        mine = buf.at[p, pl.ds(pl.multiple_of((c * B + b) * column + a * CAP, CAP), CAP)]
         return [
-            remote(mine, mine, gz_send.at[p, j], gz_recv.at[p, j], z_peers[j])
+            remote(buf.at[p, place(b, 0)], buf.at[p, place(b, A - 1 - j)], gz_send.at[p, j], gz_recv.at[p, j], z_peers[j])
             for j in range(A - 1)
         ]
 
+    def gx_own(p):
+        mine = buf.at[p, place(b, 0)]
+        return [
+            remote(mine, mine, go_send.at[p, j], go_recv.at[p, j], x_peers[j])
+            for j in range(B - 1)
+        ]
+
     def gx(p):
-        mine = buf.at[p, rows_of(b)]
+        rows = pl.ds(pl.multiple_of((c * B + b) * column + CAP, CAP), column - CAP)
+        rest = buf.at[p, rows]
         return [
-            remote(mine, mine, gx_send.at[p, j], gx_recv.at[p, j], x_peers[j])
+            remote(rest, rest, gx_send.at[p, j], gx_recv.at[p, j], x_peers[j])
             for j in range(B - 1)
         ]
 
@@ -206,9 +218,8 @@
 
     def pick(p):
         pltpu.make_async_copy(tok_ref.at[:, pl.ds(0, width)], src.at[p], src_sem.at[p]).wait()
-        rows = pl.ds(pl.multiple_of((c * B + b) * column + a * CAP, CAP), CAP)
-        buf[p, rows, :] = dot_nn(sel_ref[...], src[p]).astype(jnp.bfloat16)
-        for copy in gz(p):
+        buf[p, place(b, 0), :] = dot_nn(sel_ref[...], src[p]).astype(jnp.bfloat16)
+        for copy in gx_own(p) + gz(p):
             copy.start()
 
     def keys(p):
@@ -225,8 +236,9 @@
         gs(p, 0).start()
 
     def aside(p):
-        for j, copy in enumerate(gx(p)):
-            copy.wait_recv()
+        for j in range(B - 1):
+            gx_own(p)[j].wait_recv()
+            gx(p)[j].wait_recv()
             gs(p, B - 1 - j).start()
 
     def multiply(p):
@@ -248,10 +260,10 @@
             back_ref[...] += dot_nt(buf[p], downv[k])
 
     def sent(p):
-        for copy in gz(p) + gx(p) + [gs(p, j) for j in range(B)]:
+        for copy in gz(p) + gx_own(p) + gx(p) + [gs(p, j) for j in range(B)]:
             copy.wait_send()
 
-    staged(NP, [(0, pick), (4, across), (7, aside), (6, keys), (9, multiply), (10, sent)])
+    staged(NP, [(0, pick), (2, across), (2, keys), (4, aside), (6, multiply), (7, sent)])
 
     pre = pre_ref[...]
     sig = jax.nn.sigmoid(pre)
@@ -300,14 +312,11 @@
             total = total + x_in[q, j].astype(jnp.float32)
         part[q, mine, :] = total
         for j, copy in enumerate(rz(q)):
-            a_ = lax.rem(a + j + 1, A)
-            rows = pl.ds(pl.multiple_of(c * half + b * column + a_ * CAP, CAP), CAP)
-            z_out[q, j] = part[q, rows, :].astype(jnp.bfloat16)
+            z_out[q, j] = part[q, place(b, j + 1), :].astype(jnp.bfloat16)
             copy.start()
 
     def finish(q):
-        rows = pl.ds(pl.multiple_of(c * half + b * column + a * CAP, CAP), CAP)
-        total = part[q, rows, :]
+        total = part[q, place(b, 0), :]
         for j, copy in enumerate(rz(q)):
             copy.wait_recv()
             total = total + z_in[q, j].astype(jnp.float32)
@@ -318,7 +327,7 @@
         for copy in [rs(q)] + rx(q) + rz(q):
             copy.wait_send()
 
-    staged(KR, [(0, produce), (2, pair), (5, chain), (8, finish), (8, returned)])
+    staged(KR, [(0, produce), (1, pair), (3, chain), (5, finish), (6, returned)])
 
     def keys_done(p, carry):
         for copy in ys(p):
@@ -383,6 +392,8 @@
             dma((2 * K, A - 1)),
             dma((2 * K, B - 1)),
             dma((2 * K, B - 1)),
+            dma((2 * K, B - 1)),
+            dma((2 * K, B - 1)),
             dma((2 * K, B)),
             dma((2 * K, B)),
             dma((KR,)),

time: 87.5 us -> 81.2 us (0.928)
  Pallas kernels: 86.6 us -> 80.4 us
    pallas_call x1, Pallas kernels: 7.06 us -> 3.66 us  [tail(): pl.pallas_call(functools.partial(tail_kernel, R), grid=(G,), out_shape=(j...]
    pallas_call x1, Pallas kernels: 79.5 us -> 76.7 us  [exchange(): pl.pallas_call(functools.partial(kernel, R, A, B, K, KR), out_shape=(jax....]
where the time goes in v5:
time: 81.2 us; the launch traced here: 81 us
  Pallas kernels  80.4 us (99%)
    pallas_call x1, Pallas kernels, exchange(): pl.pallas_call(functools.partial(kernel, R, A, B, K, KR), out_shape=(jax....  76.7 us
    pallas_call x1, Pallas kernels, tail(): pl.pallas_call(functools.partial(tail_kernel, R), grid=(G,), out_shape=(j...  3.66 us

profile of v5, /device:TPU:0, one launch (start us, length us, event | category | flops | bytes accessed | tf_op | source)
XLA Modules:
  0.0 81.0 jit_solution(5145700821539251140)
XLA Ops:
  0.6 76.7 %shard_map.120 = (bf16[16,6144]{1,0:T(8,128)(2,1)}, bf16[128,128]{1,0:T(8,128)(2,1)}, f32[2,384,512]{2,1,0:T(8,128)}, f32[2,384,256]{2,1,0:T(8,128)}) custom-call(s32[2,128]{1,0:T(2,128)} %bitcast.15, f32[1,128]{1,0:T(1,128)} %share_ref.1, bf16[128,6144]{1,0:T(8,128)(2,1)} %bitcast.11, bf16[128,6144]{1,0:T(8,128)(2,1)} %bitcast.12, ...), custom_call_target="tpu_custom_call" | custom-call | flops 4831838208 | bytes 25165824 | tf_op jit(solution)/shard_map/pallas_call | solution.py:358
  77.3 3.7 %shard_map.121 = (bf16[128,6144]{1,0:T(8,128)(2,1)}, f32[384,512]{1,0:T(8,128)}, f32[384,256]{1,0:T(8,128)}, bf16[384,512]{1,0:T(8,128)(2,1)}) custom-call(bf16[128,128]{1,0:T(8,128)(2,1)} %get-tuple-element.12.sel_ref, bf16[16,6144]{1,0:T(8,128)(2,1)} %get-tuple-element.13.res_ref, f32[384,512]{1,0:T(8,128)} %outer_ref.1, ...), custom_call_target="tpu_custom_call" | custom-call | tf_op jit(solution)/shard_map/pallas_call | solution.py:445

commit v6 on v5

--- a/solution.py
+++ b/solution.py
@@ -9,8 +9,8 @@
 
 CAP = 16
 MAJOR = 4
-PIECES = 8
-BACK_PIECES = 8
+PIECES = 12
+BACK_PIECES = 12
 KEY_ROWS = 48
 TAIL_STEPS = 2
 
@@ -263,7 +263,7 @@
         for copy in gz(p) + gx_own(p) + gx(p) + [gs(p, j) for j in range(B)]:
             copy.wait_send()
 
-    staged(NP, [(0, pick), (2, across), (2, keys), (4, aside), (6, multiply), (7, sent)])
+    staged(NP, [(0, pick), (3, across), (3, keys), (5, aside), (7, multiply), (8, sent)])
 
     pre = pre_ref[...]
     sig = jax.nn.sigmoid(pre)
@@ -327,7 +327,7 @@
         for copy in [rs(q)] + rx(q) + rz(q):
             copy.wait_send()
 
-    staged(KR, [(0, produce), (1, pair), (3, chain), (5, finish), (6, returned)])
+    staged(KR, [(0, produce), (2, pair), (5, chain), (8, finish), (9, returned)])
 
     def keys_done(p, carry):
         for copy in ys(p):

time: 81.2 us -> 82.9 us (1.021)
  Pallas kernels: 80.4 us -> 82.1 us
    pallas_call x1, Pallas kernels: 76.7 us -> 78.5 us  [exchange(): pl.pallas_call(functools.partial(kernel, R, A, B, K, KR), out_shape=(jax....]
where the time goes in v6:
time: 82.9 us; the launch traced here: 82.8 us
  Pallas kernels  82.1 us (99%)
    pallas_call x1, Pallas kernels, exchange(): pl.pallas_call(functools.partial(kernel, R, A, B, K, KR), out_shape=(jax....  78.5 us
    pallas_call x1, Pallas kernels, tail(): pl.pallas_call(functools.partial(tail_kernel, R), grid=(G,), out_shape=(j...  3.66 us

profile of v6, /device:TPU:0, one launch (start us, length us, event | category | flops | bytes accessed | tf_op | source)
XLA Modules:
  0.0 82.8 jit_solution(1605630915303270727)
XLA Ops:
  0.6 78.5 %shard_map.120 = (bf16[16,6144]{1,0:T(8,128)(2,1)}, bf16[128,128]{1,0:T(8,128)(2,1)}, f32[2,384,512]{2,1,0:T(8,128)}, f32[2,384,256]{2,1,0:T(8,128)}) custom-call(s32[2,128]{1,0:T(2,128)} %bitcast.15, f32[1,128]{1,0:T(1,128)} %share_ref.1, bf16[128,6144]{1,0:T(8,128)(2,1)} %bitcast.11, bf16[128,6144]{1,0:T(8,128)(2,1)} %bitcast.12, ...), custom_call_target="tpu_custom_call" | custom-call | flops 4831838208 | bytes 25165824 | tf_op jit(solution)/shard_map/pallas_call | solution.py:358
  79.1 3.7 %shard_map.121 = (bf16[128,6144]{1,0:T(8,128)(2,1)}, f32[384,512]{1,0:T(8,128)}, f32[384,256]{1,0:T(8,128)}, bf16[384,512]{1,0:T(8,128)(2,1)}) custom-call(bf16[128,128]{1,0:T(8,128)(2,1)} %get-tuple-element.12.sel_ref, bf16[16,6144]{1,0:T(8,128)(2,1)} %get-tuple-element.13.res_ref, f32[384,512]{1,0:T(8,128)} %outer_ref.1, ...), custom_call_target="tpu_custom_call" | custom-call | tf_op jit(solution)/shard_map/pallas_call | solution.py:445

commit v7 on v5

--- a/solution.py
+++ b/solution.py
@@ -10,9 +10,9 @@
 CAP = 16
 MAJOR = 4
 PIECES = 8
-BACK_PIECES = 8
+BACK_PIECES = 6
 KEY_ROWS = 48
-TAIL_STEPS = 2
+TAIL_STEPS = 1
 
 outer_beta = 0.9
 outer_rate = 0.7
@@ -327,7 +327,7 @@
         for copy in [rs(q)] + rx(q) + rz(q):
             copy.wait_send()
 
-    staged(KR, [(0, produce), (1, pair), (3, chain), (5, finish), (6, returned)])
+    staged(KR, [(0, produce), (1, pair), (2, chain), (4, finish), (5, returned)])
 
     def keys_done(p, carry):
         for copy in ys(p):

time: 81.2 us -> 82.6 us (1.017)
  Pallas kernels: 80.4 us -> 81.7 us
    pallas_call x1, Pallas kernels: 3.66 us -> 4.62 us  [tail(): pl.pallas_call(functools.partial(tail_kernel, R), grid=(G,), out_shape=(j...]
where the time goes in v7:
time: 82.6 us; the launch traced here: 82.4 us
  Pallas kernels  81.7 us (99%)
    pallas_call x1, Pallas kernels, exchange(): pl.pallas_call(functools.partial(kernel, R, A, B, K, KR), out_shape=(jax....  77.1 us
    pallas_call x1, Pallas kernels, tail(): pl.pallas_call(functools.partial(tail_kernel, R), grid=(G,), out_shape=(j...  4.62 us

profile of v7, /device:TPU:0, one launch (start us, length us, event | category | flops | bytes accessed | tf_op | source)
XLA Modules:
  0.0 82.4 jit_solution(9032032988305304406)
XLA Ops:
  0.6 77.1 %shard_map.120 = (bf16[16,6144]{1,0:T(8,128)(2,1)}, bf16[128,128]{1,0:T(8,128)(2,1)}, f32[2,384,512]{2,1,0:T(8,128)}, f32[2,384,256]{2,1,0:T(8,128)}) custom-call(s32[2,128]{1,0:T(2,128)} %bitcast.15, f32[1,128]{1,0:T(1,128)} %share_ref.1, bf16[128,6144]{1,0:T(8,128)(2,1)} %bitcast.11, bf16[128,6144]{1,0:T(8,128)(2,1)} %bitcast.12, ...), custom_call_target="tpu_custom_call" | custom-call | flops 4831838208 | bytes 25165824 | tf_op jit(solution)/shard_map/pallas_call | solution.py:358
  77.8 4.6 %shard_map.121 = (bf16[128,6144]{1,0:T(8,128)(2,1)}, f32[384,512]{1,0:T(8,128)}, f32[384,256]{1,0:T(8,128)}, bf16[384,512]{1,0:T(8,128)(2,1)}) custom-call(bf16[128,128]{1,0:T(8,128)(2,1)} %get-tuple-element.12.sel_ref, bf16[16,6144]{1,0:T(8,128)(2,1)} %get-tuple-element.13.res_ref, f32[384,512]{1,0:T(8,128)} %outer_ref.1, ...), custom_call_target="tpu_custom_call" | custom-call | tf_op jit(solution)/shard_map/pallas_call | solution.py:445
